TPU v7x, 32 devices: a whole 2x2x4 slice. The times are simulated.
32 devices in a mesh: parts: 2 (over y), dp: 4 (over z), tensor: 4 (over x, core).
Axes of the slice: x: 2, y: 2, z: 4, core: 2. Of those that a mesh axis runs over, the one named last changes fastest.
Arguments:
- queries: bfloat16 [6144, 6144], P(('parts', 'dp'), 'tensor'), parts along dimension 0, may hold values from -6 to 6
- keys: bfloat16 [6144, 6144], P(('parts', 'dp'), 'tensor'), parts along dimension 0, may hold values from -8 to 8
- values: bfloat16 [6144, 6144], P(('parts', 'dp'), 'tensor'), parts along dimension 0, may hold values from -6 to 6
- segment: int32 [6144], P(('parts', 'dp')), parts along dimension 0, may hold values from 0 to 23, as said below
- w_out: bfloat16 [6144, 5120], P('tensor'), may hold values from -0.109375 to 0.109375
- w_scale: float32 [48, 40], P('tensor'), may hold values from 0.25 to 4
- handover: int32 [6], P('parts'), parts along dimension 0, may hold values from 0 to 3, as said below
Outputs:
- handed: bfloat16 [5120, 6144], P('tensor', ('parts', 'dp')), parts along dimension 1
There are 2 independent parts, one for each index of `parts`. A program takes and returns all parts, laid end to end along the dimension named above; an argument that names none is the same for every part. Nothing has to cross between parts.
Inputs may be any that keep to these rules, and one draw needn't show every extreme that they name: Within each group's 768 rows the segment numbers start at 0, never fall and rise by at most one from row to row; a new sequence starts only at a multiple of 32 rows, and always at each multiple of 256 rows past the first. `handover`: every distance appears at most 1 times, and some distance exactly 1 times.
All inputs are finite; a program needn't handle non-finite values.
Results may differ from a plain program's by a relative error of at most 0.0095.
Values may be sent and summed in bfloat16 or wider, within the bound.
No kernel may reach another device: no remote copies, remote signals or barrier semaphores. Data moves between devices by JAX's collectives and lax.ppermute only.
A program may use at most 192 MiB of HBM per device.

v0:
```python
import functools

import jax
import jax.numpy as jnp
from jax import lax
from jax.experimental import pallas as pl
from jax.experimental.pallas import tpu as pltpu
from jax.sharding import PartitionSpec as P

HD = 128
PIECE = 256
WIDE = 256
NEG = -1e30
LOG2E = 1.4426950408889634
VMEM = 16 * 1024 * 1024
HEADS_STEP = 4

ANY = pl.BlockSpec(memory_space=pl.ANY)


def params():
    return pltpu.CompilerParams(vmem_limit_bytes=VMEM)


def attend_heads(heads, q_ref, k_ref, v_ref, bias, o_ref, first=0):
    ones = jnp.ones((PIECE, HD), jnp.bfloat16)
    for h in range(first, first + heads):
        cols = slice(h * HD, (h + 1) * HD)
        scores = lax.dot_general(
            q_ref[:, cols], k_ref[:, cols], (((1,), (1,)), ((), ())), preferred_element_type=jnp.float32
        )
        scores = scores * (LOG2E * HD ** -0.5) + bias
        top = jnp.max(scores, axis=1, keepdims=True)
        weights = jnp.exp2(scores - top).astype(jnp.bfloat16)
        both = jnp.concatenate([v_ref[:, cols], ones], axis=1)
        mixed = jnp.dot(weights, both, preferred_element_type=jnp.float32)
        o_ref[:, cols] = (mixed[:, :HD] / mixed[:, HD:]).astype(jnp.bfloat16)


def segment_bias(numbers):
    across = jnp.broadcast_to(numbers.astype(jnp.float32), (PIECE, PIECE))
    return jnp.where(across == jnp.transpose(across), 0.0, NEG)


def missing(meta_ref):
    return 6 - (meta_ref[1] + meta_ref[2] + meta_ref[3])


def slot_distance(meta_ref, slot):
    gone = missing(meta_ref)
    passed = gone == SHIFTS[0]
    for shift in SHIFTS[1:slot + 1]:
        passed = jnp.logical_or(passed, gone == shift)
    return jnp.where(passed, (SHIFTS + (0,))[slot + 1], SHIFTS[slot])


def piece_at(meta_ref, distance):
    piece = jnp.where(meta_ref[1] == distance, 0, jnp.where(meta_ref[2] == distance, 1, 2))
    return pl.multiple_of(piece * PIECE, PIECE)


def scaled_product(a_ref, w_ref, s_ref, local_col, global_col):
    rows = []
    for kb in range(w_ref.shape[0] // HD):
        blocks = []
        for fb in range(WIDE // HD):
            tile = w_ref[kb * HD:(kb + 1) * HD, local_col + fb * HD:local_col + (fb + 1) * HD]
            scale = s_ref[kb, global_col // HD + fb]
            blocks.append((tile.astype(jnp.float32) * scale).astype(jnp.bfloat16))
        rows.append(jnp.concatenate(blocks, axis=1))
    return jnp.dot(a_ref[...], jnp.concatenate(rows, axis=0), preferred_element_type=jnp.float32)


def spans(me, features, flip, ranges):
    away, home = (me ^ 2) ^ flip, me ^ flip
    return [
        (pl.multiple_of(rank * features + first, HD), width) for first, width in ranges for rank in (away, home)
    ]


def sibling_kernel(features, slot, ranges, cut, attend, meta_ref, *refs):
    refs = list(refs)
    inputs = [refs.pop(0) for _ in range(7 if attend else 4)]
    outs = [refs.pop(0) for _ in range(sum(len(pieces_of(width, cut)) for _, width in ranges))]
    if attend:
        q_hbm, k_hbm, v_hbm, seg_hbm, w_hbm, s_hbm, _ = inputs
        att_hbm = refs.pop(0)
        att, w_ref, s_ref, out, w_sem, o_sem, s_sem, q_ref, k_ref, v_ref, seg_ref, in_sem, seg_sem, att_sem = refs
        first_row = piece_at(meta_ref, slot_distance(meta_ref, slot))
        groups = q_ref.shape[1] // (HEADS_STEP * HD)
        loads = []
        seg_load = pltpu.make_async_copy(seg_hbm.at[pl.ds(first_row // PIECE, 1)], seg_ref, seg_sem)
        seg_load.start()
        for g in range(groups):
            cols = pl.ds(g * HEADS_STEP * HD, HEADS_STEP * HD)
            for i, (source, dest) in enumerate(((q_hbm, q_ref), (k_hbm, k_ref), (v_hbm, v_ref))):
                load = pltpu.make_async_copy(
                    source.at[pl.ds(first_row, PIECE), cols], dest.at[:, cols], in_sem.at[g, i]
                )
                load.start()
                loads.append(load)
    else:
        att_hbm, w_hbm, s_hbm, _ = inputs
        att, w_ref, s_ref, out, w_sem, o_sem, s_sem, att_sem = refs
        att_load = pltpu.make_async_copy(att_hbm, att, att_sem)
        att_load.start()
    scale_load = pltpu.make_async_copy(s_hbm, s_ref, s_sem)
    scale_load.start()
    columns = spans(meta_ref[0], features, 1, ranges)
    w_loads, at = [], 0
    for i, (first, width) in enumerate(columns):
        load = pltpu.make_async_copy(w_hbm.at[:, pl.ds(first, width)], w_ref.at[:, pl.ds(at, width)], w_sem.at[i])
        load.start()
        w_loads.append(load)
        at += width
    if attend:
        seg_load.wait()
        bias = segment_bias(seg_ref[0])
        for g in range(groups):
            for load in loads[3 * g:3 * g + 3]:
                load.wait()
            attend_heads(HEADS_STEP, q_ref, k_ref, v_ref, bias, att, g * HEADS_STEP)
        att_store = pltpu.make_async_copy(att, att_hbm, att_sem)
        att_store.start()
    else:
        att_load.wait()
    scale_load.wait()
    stores, at, done = [], 0, 0
    for i, (first, width) in enumerate(columns):
        w_loads[i].wait()
        for inner in range(0, width, WIDE):
            product = scaled_product(att, w_ref, s_ref, at + inner, first + inner)
            out[:, at + inner:at + inner + WIDE] = product.astype(jnp.bfloat16)
        at += width
        if i % 2:
            for piece in pieces_of(width, cut):
                dest = outs[len(stores)]
                store = pltpu.make_async_copy(out.at[:, pl.ds(done, piece)], dest, o_sem.at[len(stores)])
                store.start()
                stores.append(store)
                done += piece
    for store in stores:
        store.wait()
    if attend:
        att_store.wait()


def pieces_of(width, cut):
    return [2 * width] if cut is None else [cut] * (2 * width // cut)


def sibling_part(meta, slot, ranges, cut, inputs, attended, w_out, w_scale, features, token, cost):
    rows, depth = PIECE, w_out.shape[0]
    widths = [piece for _, width in ranges for piece in pieces_of(width, cut)]
    attend = attended is None
    bf16 = jnp.bfloat16
    scratch = [
        pltpu.VMEM((rows, depth), bf16),
        pltpu.VMEM((depth, sum(widths)), bf16),
        pltpu.SMEM(w_scale.shape, jnp.float32),
        pltpu.VMEM((rows, sum(widths)), bf16),
        pltpu.SemaphoreType.DMA((2 * len(ranges),)),
        pltpu.SemaphoreType.DMA((len(widths),)),
        pltpu.SemaphoreType.DMA,
    ]
    shapes = [jax.ShapeDtypeStruct((rows, width), bf16) for width in widths]
    if attend:
        scratch += [pltpu.VMEM((rows, depth), bf16)] * 3
        scratch += [pltpu.VMEM((1, 1, PIECE), jnp.int32)]
        scratch += [pltpu.SemaphoreType.DMA((depth // (HEADS_STEP * HD), 3)), pltpu.SemaphoreType.DMA]
        shapes.append(jax.ShapeDtypeStruct((rows, depth), bf16))
    operands = (tuple(inputs) if attend else (attended,)) + (w_out, w_scale, token)
    result = pl.pallas_call(
        functools.partial(sibling_kernel, features, slot, ranges, cut, attend),
        grid_spec=pltpu.PrefetchScalarGridSpec(
            num_scalar_prefetch=1,
            grid=(1,),
            in_specs=[ANY] * len(operands),
            out_specs=[ANY] * len(shapes),
            scratch_shapes=scratch + [pltpu.SemaphoreType.DMA],
        ),
        out_shape=shapes,
        compiler_params=params(),
        cost_estimate=cost,
    )(meta, *operands)
    parts, at = [], 0
    for _, width in ranges:
        count = len(pieces_of(width, cut))
        parts.append(result[at:at + count])
        at += count
    return parts, result[-1] if attend else attended


def own_kernel(features, chunk, count, meta_ref, att_hbm, w_hbm, s_hbm, *refs):
    received, refs = refs[:count], refs[count + 1:]
    send_hbm, keep_hbm, att, w_ref, s_ref, r_ref, out, w_sem, r_sem, o_sem, s_sem, att_sem = refs
    width = chunk[1]
    att_load = pltpu.make_async_copy(att_hbm, att, att_sem)
    att_load.start()
    scale_load = pltpu.make_async_copy(s_hbm, s_ref, s_sem)
    scale_load.start()
    columns = spans(meta_ref[0], features, 0, [chunk])
    loads, at = [], 0
    for i, (first, _) in enumerate(columns):
        load = pltpu.make_async_copy(
            w_hbm.at[:, pl.ds(first, width)], w_ref.at[:, pl.ds(i * width, width)], w_sem.at[i]
        )
        load.start()
        loads.append(load)
    received_loads = []
    for i, source in enumerate(received):
        load = pltpu.make_async_copy(source, r_ref.at[:, pl.ds(at, source.shape[1])], r_sem.at[i])
        load.start()
        received_loads.append(load)
        at += source.shape[1]
    att_load.wait()
    scale_load.wait()
    for load in received_loads:
        load.wait()
    stores = []
    for i, (first, _) in enumerate(columns):
        loads[i].wait()
        for inner in range(0, width, WIDE):
            cols = slice(i * width + inner, i * width + inner + WIDE)
            product = scaled_product(att, w_ref, s_ref, i * width + inner, first + inner)
            out[:, cols] = (product + r_ref[:, cols].astype(jnp.float32)).astype(jnp.bfloat16)
        store = pltpu.make_async_copy(out.at[:, pl.ds(i * width, width)], (send_hbm, keep_hbm)[i], o_sem.at[i])
        store.start()
        stores.append(store)
    for store in stores:
        store.wait()


def own_part(meta, chunk, attended, w_out, w_scale, received, features, token, cost):
    rows, depth = attended.shape
    width = chunk[1]
    bf16 = jnp.bfloat16
    return pl.pallas_call(
        functools.partial(own_kernel, features, chunk, len(received)),
        grid_spec=pltpu.PrefetchScalarGridSpec(
            num_scalar_prefetch=1,
            grid=(1,),
            in_specs=[ANY] * (4 + len(received)),
            out_specs=[ANY] * 2,
            scratch_shapes=[
                pltpu.VMEM((rows, depth), bf16),
                pltpu.VMEM((depth, 2 * width), bf16),
                pltpu.SMEM(w_scale.shape, jnp.float32),
                pltpu.VMEM((rows, 2 * width), bf16),
                pltpu.VMEM((rows, 2 * width), bf16),
                pltpu.SemaphoreType.DMA((2,)),
                pltpu.SemaphoreType.DMA((len(received),)),
                pltpu.SemaphoreType.DMA((2,)),
                pltpu.SemaphoreType.DMA,
                pltpu.SemaphoreType.DMA,
            ],
        ),
        out_shape=[jax.ShapeDtypeStruct((rows, width), bf16)] * 2,
        compiler_params=params(),
        cost_estimate=cost,
    )(meta, attended, w_out, w_scale, *received, token)


def finish_kernel(slot, first, into, arrivals, meta_ref, *refs):
    refs = list(refs)
    sem, out = refs.pop(), refs.pop()
    whole = refs.pop() if into else None
    pair = [refs.pop(0), refs.pop(0)] if slot is not None else []
    before = refs.pop(0) if slot else None
    stores = []
    for i, (shift, at) in enumerate(arrivals):
        source = refs.pop(0)
        dest = whole.at[pl.ds(at, source.shape[0]), pl.ds(piece_at(meta_ref, shift), PIECE)]
        stores.append((missing(meta_ref) != shift, pltpu.make_async_copy(source, dest, sem.at[3 + i])))
    for exists, store in stores:
        pl.when(exists)(store.start)
    if slot is not None:
        keep_ref, r_ref = pair
        width = keep_ref.shape[1]
        for at in range(0, width, WIDE):
            cols = slice(at, at + WIDE)
            total = keep_ref[:, cols].astype(jnp.float32) + r_ref[:, cols].astype(jnp.float32)
            out[cols, :] = jnp.transpose(total.astype(jnp.bfloat16))
        last = slot == len(SHIFTS) - 1
        results = refs[-2:] if slot and not last else refs[-1:]
        sent = results[0]
        own = pltpu.make_async_copy(out, sent, sem.at[0])
        if slot == 0:
            own.start()
        else:
            moved = slot_distance(meta_ref, slot) == SHIFTS[slot]
            pl.when(moved)(own.start)
            pl.when(jnp.logical_not(moved))(pltpu.make_async_copy(before, sent, sem.at[0]).start)
        if slot and not last:
            copy = pltpu.make_async_copy(out, results[1], sem.at[1])
            copy.start()
            copy.wait()
        if last:
            dest = whole.at[pl.ds(first, width), pl.ds(piece_at(meta_ref, 0), PIECE)]
            stay = pltpu.make_async_copy(out, dest, sem.at[2])
            pl.when(jnp.logical_not(moved))(stay.start)
            pl.when(jnp.logical_not(moved))(stay.wait)
        own.wait()
    for exists, store in stores:
        pl.when(exists)(store.wait)


def finish(meta, slot, first, pair, before, arrivals, whole, target, token, cost):
    last = slot == len(SHIFTS) - 1
    into = bool(arrivals) or last
    arrays = list(pair) + ([before] if slot else []) + [chunk for _, _, chunk in arrivals]
    specs = [pl.BlockSpec(array.shape, lambda g, meta: (0, 0)) for array in arrays]
    if token is not whole:
        arrays, specs = arrays + [token], specs + [ANY]
    aliases = {}
    scratch_shape = (pair[0].shape[1], PIECE) if pair else (16, HD)
    shapes = []
    if slot is not None:
        shapes = [jax.ShapeDtypeStruct(scratch_shape, jnp.bfloat16)] * (2 if slot and not last else 1)
    if into:
        if whole is not None:
            aliases = {1 + len(arrays): len(shapes)}
            arrays, specs = arrays + [whole], specs + [ANY]
        shapes.append(target)
    result = pl.pallas_call(
        functools.partial(finish_kernel, slot, first, into, [a[:2] for a in arrivals]),
        grid_spec=pltpu.PrefetchScalarGridSpec(
            num_scalar_prefetch=1,
            grid=(1,),
            in_specs=specs,
            out_specs=[ANY] * len(shapes),
            scratch_shapes=[
                pltpu.VMEM(scratch_shape, jnp.bfloat16), pltpu.SemaphoreType.DMA((3 + len(arrivals),))
            ],
        ),
        out_shape=shapes,
        input_output_aliases=aliases,
        compiler_params=params(),
        cost_estimate=cost,
    )(meta, *arrays)
    sent = result[0] if slot is not None else None
    return sent, result[1] if slot and not last else sent, result[-1] if into else whole


SHORT = pl.CostEstimate(flops=1000, bytes_accessed=1000, transcendentals=0)
LONG = pl.CostEstimate(flops=5 * 10**10, bytes_accessed=1000, transcendentals=0)

SHIFTS = (2, 1, 3)
CHUNKS = ((0, 0, 768), (0, 768, 512), (1, 0, 768), (1, 768, 512), (2, 0, 768), (2, 768, 512))
SHARES = ((0, (0, 1)), (1, (2, 3)), (2, (4, 5)))
CUT = None
STEPS = (
    "s0", "o0", "s1", "f0", "o3", "o2", "p0", "o1", "s2", "f1", "o4", "f2", "p1", "f3", "p2", "o5", "f4",
    "p3", "f5", "p4", "p5",
)
COUNT_LONG = ("f0", "f1", "f3", "f4", "f5",)


def pipeline(meta, queries, keys, values, segment, w_out, w_scale):
    groups = lax.axis_size("dp")
    ranks = lax.axis_size("tensor")
    features = w_out.shape[1] // ranks
    other_core = [(i, i ^ 1) for i in range(ranks)]
    other_chip = [(i, i ^ 2) for i in range(ranks)]
    target = jax.ShapeDtypeStruct((features, queries.shape[0]), jnp.bfloat16)
    inputs = (queries, keys, values, segment)
    attended, from_core, kept, from_chip, finished, arrived = {}, {}, {}, {}, {}, {}
    token, whole, waiting = meta, None, []
    finishes = sum(step[0] == "f" for step in STEPS)

    for step in STEPS:
        kind, index = step[0], int(step[1:])
        cost = LONG if step in COUNT_LONG else SHORT
        if kind == "s":
            slot, members = SHARES[index]
            ranges = [CHUNKS[i][1:] for i in members]
            parts, attended[slot] = sibling_part(
                meta, slot, ranges, CUT, inputs, attended.get(slot), w_out, w_scale, features, token, cost
            )
            token = parts[0][0]
            for i, arrays in zip(members, parts):
                from_core[i] = [lax.ppermute(array, "tensor", other_core) for array in arrays]
            continue
        slot, first, width = CHUNKS[index]
        if kind == "o":
            send, kept[index] = own_part(
                meta, (first, width), attended[slot], w_out, w_scale, from_core[index], features, token, cost
            )
            token = kept[index]
            from_chip[index] = lax.ppermute(send, "tensor", other_chip)
            continue
        if kind == "p":
            waiting.append((SHIFTS[slot], first, arrived[index]))
            if finishes:
                continue
            _, _, whole = finish(meta, None, first, (), None, waiting, whole, target, token, cost)
            token, waiting = whole, []
            continue
        finishes -= 1
        pair, before = (kept[index], from_chip[index]), finished.get((slot - 1, first))
        token, finished[slot, first], whole = finish(
            meta, slot, first, pair, before, waiting, whole, target, token, cost
        )
        waiting = []
        arrived[index] = lax.ppermute(token, "dp", [(i, (i + SHIFTS[slot]) % groups) for i in range(groups)])
    return whole


def attention_kernel(heads, q_ref, k_ref, v_ref, seg_ref, o_ref):
    attend_heads(heads, q_ref, k_ref, v_ref, segment_bias(seg_ref[0]), o_ref)


def attend_all(queries, keys, values, segment):
    rows, width = queries.shape
    heads = HEADS_STEP if (width // HD) % HEADS_STEP == 0 else 1
    block = pl.BlockSpec((PIECE, heads * HD), lambda i, g: (i, g))
    return pl.pallas_call(
        functools.partial(attention_kernel, heads),
        grid=(rows // PIECE, width // (heads * HD)),
        in_specs=[block, block, block, pl.BlockSpec((1, 1, PIECE), lambda i, g: (i, 0, 0))],
        out_specs=block,
        out_shape=jax.ShapeDtypeStruct((rows, width), jnp.bfloat16),
        compiler_params=params(),
    )(queries, keys, values, segment)


def general(queries, keys, values, segment, w_out, w_scale, handover):
    row_count, width = queries.shape
    piece_count = handover.shape[0]
    groups, my_group = lax.axis_size("dp"), lax.axis_index("dp")
    attended = attend_all(queries, keys, values, segment.reshape(-1, 1, PIECE))
    scale_rows, scale_cols = w_scale.shape
    blocked = w_out.astype(jnp.float32).reshape(scale_rows, HD, scale_cols, w_out.shape[1] // scale_cols)
    weight = (blocked * w_scale[:, None, :, None]).reshape(w_out.shape).astype(jnp.bfloat16)
    partial = lax.dot_general(weight, attended, (((0,), (1,)), ((), ())), preferred_element_type=jnp.float32)
    home = lax.psum_scatter(partial.astype(jnp.bfloat16), "tensor", scatter_dimension=0, tiled=True)
    pieces = home.reshape(home.shape[0], piece_count, PIECE)
    slots = jnp.arange(groups, dtype=jnp.int32)
    goes = (jnp.mod(my_group + handover, groups)[None, :] == slots[:, None]).astype(jnp.bfloat16)
    comes = (jnp.mod(my_group - handover, groups)[:, None] == slots[None, :]).astype(jnp.bfloat16)
    outgoing = jnp.einsum("tj,cjp->tcp", goes, pieces, preferred_element_type=jnp.float32).astype(jnp.bfloat16)
    arrived = lax.all_to_all(outgoing, "dp", split_axis=0, concat_axis=0, tiled=True)
    handed = jnp.einsum("jt,tcp->cjp", comes, arrived, preferred_element_type=jnp.float32).astype(jnp.bfloat16)
    return handed.reshape(home.shape[0], row_count)


def local(queries, keys, values, segment, w_out, w_scale, handover):
    fits = (
        lax.axis_size("dp") == 4
        and lax.axis_size("tensor") == 4
        and handover.shape[0] == 3
        and w_out.shape == (1536, 4 * 1280)
        and queries.shape[0] == 3 * PIECE
    )
    if not fits:
        return general(queries, keys, values, segment, w_out, w_scale, handover)
    meta = jnp.concatenate([lax.axis_index("tensor").astype(jnp.int32)[None], handover])
    return pipeline(meta, queries, keys, values, segment.reshape(-1, 1, PIECE), w_out, w_scale)


def solution(mesh):
    return jax.shard_map(
        local,
        mesh=mesh,
        in_specs=(
            P(("parts", "dp"), "tensor"),
            P(("parts", "dp"), "tensor"),
            P(("parts", "dp"), "tensor"),
            P(("parts", "dp")),
            P("tensor", None),
            P("tensor", None),
            P("parts"),
        ),
        out_specs=P("tensor", ("parts", "dp")),
        check_vma=False,
    )
```

profile of v0, /device:TPU:0, one launch (start us, length us, event | category | flops | bytes accessed | tf_op | source)
XLA Modules:
  0.0 111.8 jit_solution(12011862683719360126)
XLA Ops:
  1.4 5.5 %copy-done = bf16[1536,5120]{1,0:T(8,128)(2,1)S(1)} copy-done((bf16[1536,5120]{1,0:T(8,128)(2,1)S(1)}, bf16[1536,5120]{1,0:T(8,128)(2,1)}, u32[]{:S(2)}) %copy-start) | copy-done | bytes 15728664
  6.9 1.7 %copy-done.2 = bf16[768,1536]{1,0:T(8,128)(2,1)S(1)} copy-done((bf16[768,1536]{1,0:T(8,128)(2,1)S(1)}, bf16[768,1536]{1,0:T(8,128)(2,1)}, u32[]{:S(2)}) %copy-start.2) | copy-done | bytes 2359320
  8.6 1.7 %copy-done.4 = bf16[768,1536]{1,0:T(8,128)(2,1)S(1)} copy-done((bf16[768,1536]{1,0:T(8,128)(2,1)S(1)}, bf16[768,1536]{1,0:T(8,128)(2,1)}, u32[]{:S(2)}) %copy-start.4) | copy-done | bytes 2359320
  10.2 1.7 %copy-done.5 = bf16[768,1536]{1,0:T(8,128)(2,1)S(1)} copy-done((bf16[768,1536]{1,0:T(8,128)(2,1)S(1)}, bf16[768,1536]{1,0:T(8,128)(2,1)}, u32[]{:S(2)}) %copy-start.5) | copy-done | bytes 2359320
  12.6 7.3 %shard_map.73 = (bf16[256,1536]{1,0:T(8,128)(2,1)S(1)}, bf16[256,1024]{1,0:T(8,128)(2,1)S(1)}, bf16[256,1536]{1,0:T(8,128)(2,1)S(1)}) custom-call(s32[4]{0:T(128)S(1)} %pad_add_fusion.meta_ref.refs_6_, bf16[768,1536]{1,0:T(8,128)(2,1)S(1)} %copy-done.2, bf16[768,1536]{1,0:T(8,128)(2,1)S(1)} %copy-done.4, bf16[768,1536]{1,0:T(8,128)(2,1)S(1)} %copy-done.5, ...), custom_call_target="tpu_custom_call" | custom-call | flops 1000 | bytes 1000 | tf_op jit(solution)/shard_map/pallas_call | solution.py:173
  20.4 1.9 %collective-permute-done.1.refs_0_ = bf16[256,1536]{1,0:T(8,128)(2,1)S(1)} collective-permute-done((bf16[256,1536]{1,0:T(8,128)(2,1)S(1)}, bf16[256,1536]{1,0:T(8,128)(2,1)S(1)}, u32[]{:S(2)}, u32[]{:S(2)}) %collective-permute-start.1) | collective-permute-done | bytes 786464 | tf_op jit(solution)/shard_map/ppermute | solution.py:382
  22.3 3.4 %shard_map.74 = (bf16[256,768]{1,0:T(8,128)(2,1)S(1)}, bf16[256,768]{1,0:T(8,128)(2,1)S(1)}) custom-call(s32[4]{0:T(128)S(1)} %pad_add_fusion.meta_ref.refs_6_, bf16[256,1536]{1,0:T(8,128)(2,1)S(1)} %get-tuple-element.37.att_hbm, bf16[1536,5120]{1,0:T(8,128)(2,1)S(1)} %copy-done.1, f32[12,40]{1,0:T(8,128)S(1)} %copy-done.6, ...), custom_call_target="tpu_custom_call" | custom-call | flops 1000 | bytes 1000 | tf_op jit(solution)/shard_map/pallas_call | solution.py:238
  25.7 2.9 %collective-permute-start.4 = (bf16[256,768]{1,0:T(8,128)(2,1)S(1)}, bf16[256,768]{1,0:T(8,128)(2,1)S(1)}, u32[]{:S(2)}, u32[]{:S(2)}) collective-permute-start(bf16[256,768]{1,0:T(8,128)(2,1)S(1)} %get-tuple-element.44), channel_id=1, source_target_pairs={{0,2},{1,3},{2,0},{3,1},{4,6},{5,7},{6,4},{7,5},{8,10},{9,11},{10,... | collective-permute-start | bytes 1179656 | tf_op jit(solution)/shard_map/ppermute | solution.py:390
  28.6 7.4 %shard_map.75 = (bf16[256,1536]{1,0:T(8,128)(2,1)S(1)}, bf16[256,1024]{1,0:T(8,128)(2,1)S(1)}, bf16[256,1536]{1,0:T(8,128)(2,1)S(1)}) custom-call(s32[4]{0:T(128)S(1)} %pad_add_fusion.meta_ref.refs_6_, bf16[768,1536]{1,0:T(8,128)(2,1)S(1)} %copy-done.2, bf16[768,1536]{1,0:T(8,128)(2,1)S(1)} %copy-done.4, bf16[768,1536]{1,0:T(8,128)(2,1)S(1)} %copy-done.5, ...), custom_call_target="tpu_custom_call" | custom-call | flops 1000 | bytes 1000 | tf_op jit(solution)/shard_map/pallas_call | solution.py:173
  36.7 1.3 %collective-permute-done.4.refs_1_ = bf16[256,768]{1,0:T(8,128)(2,1)S(1)} collective-permute-done((bf16[256,768]{1,0:T(8,128)(2,1)S(1)}, bf16[256,768]{1,0:T(8,128)(2,1)S(1)}, u32[]{:S(2)}, u32[]{:S(2)}) %collective-permute-start.4) | collective-permute-done | bytes 393248 | tf_op jit(solution)/shard_map/ppermute | solution.py:390
  39.0 2.9 %collective-permute-start.8 = (bf16[768,256]{1,0:T(8,128)(2,1)S(1)}, bf16[768,256]{1,0:T(8,128)(2,1)S(1)}, u32[]{:S(2)}, u32[]{:S(2)}) collective-permute-start(bf16[768,256]{1,0:T(8,128)(2,1)S(1)} %shard_map.76.refs_1_.refs_2_), channel_id=1, source_target_pairs={{0,8},{4,12},{8,0},{12,4},{1,9},{5,13},{9,1},{13,5},{2,10},{6,14},... | collective-permute-start | bytes 1179656 | tf_op jit(solution)/shard_map/ppermute | solution.py:405
  41.9 2.5 %shard_map.77 = (bf16[256,512]{1,0:T(8,128)(2,1)S(1)}, bf16[256,512]{1,0:T(8,128)(2,1)S(1)}) custom-call(s32[4]{0:T(128)S(1)} %pad_add_fusion.meta_ref.refs_6_, bf16[256,1536]{1,0:T(8,128)(2,1)S(1)} %get-tuple-element.41.att_hbm, bf16[1536,5120]{1,0:T(8,128)(2,1)S(1)} %copy-done.1, f32[12,40]{1,0:T(8,128)S(1)} %copy-done.6, ...), custom_call_target="tpu_custom_call" | custom-call | flops 1000 | bytes 1000 | tf_op jit(solution)/shard_map/pallas_call | solution.py:238
  44.4 3.4 %shard_map.78 = (bf16[256,768]{1,0:T(8,128)(2,1)S(1)}, bf16[256,768]{1,0:T(8,128)(2,1)S(1)}) custom-call(s32[4]{0:T(128)S(1)} %pad_add_fusion.meta_ref.refs_6_, bf16[256,1536]{1,0:T(8,128)(2,1)S(1)} %get-tuple-element.41.att_hbm, bf16[1536,5120]{1,0:T(8,128)(2,1)S(1)} %copy-done.1, f32[12,40]{1,0:T(8,128)S(1)} %copy-done.6, ...), custom_call_target="tpu_custom_call" | custom-call | flops 1000 | bytes 1000 | tf_op jit(solution)/shard_map/pallas_call | solution.py:238
  47.8 2.5 %shard_map.79 = (bf16[256,512]{1,0:T(8,128)(2,1)S(1)}, bf16[256,512]{1,0:T(8,128)(2,1)S(1)}) custom-call(s32[4]{0:T(128)S(1)} %pad_add_fusion.meta_ref.refs_6_, bf16[256,1536]{1,0:T(8,128)(2,1)S(1)} %get-tuple-element.37.att_hbm, bf16[1536,5120]{1,0:T(8,128)(2,1)S(1)} %copy-done.1, f32[12,40]{1,0:T(8,128)S(1)} %copy-done.6, ...), custom_call_target="tpu_custom_call" | custom-call | flops 1000 | bytes 1000 | tf_op jit(solution)/shard_map/pallas_call | solution.py:238
  50.4 1.5 %collective-permute-start.7 = (bf16[256,512]{1,0:T(8,128)(2,1)S(1)}, bf16[256,512]{1,0:T(8,128)(2,1)S(1)}, u32[]{:S(2)}, u32[]{:S(2)}) collective-permute-start(bf16[256,512]{1,0:T(8,128)(2,1)S(1)} %get-tuple-element.51), channel_id=1, source_target_pairs={{0,2},{1,3},{2,0},{3,1},{4,6},{5,7},{6,4},{7,5},{8,10},{9,11},{10,... | collective-permute-start | bytes 786440 | tf_op jit(solution)/shard_map/ppermute | solution.py:390
  52.4 1.5 %collective-permute-start.10 = (bf16[256,768]{1,0:T(8,128)(2,1)S(1)}, bf16[256,768]{1,0:T(8,128)(2,1)S(1)}, u32[]{:S(2)}, u32[]{:S(2)}) collective-permute-start(bf16[256,768]{1,0:T(8,128)(2,1)S(1)} %get-tuple-element.54), channel_id=1, source_target_pairs={{0,2},{1,3},{2,0},{3,1},{4,6},{5,7},{6,4},{7,5},{8,10},{9,11},{10,... | collective-permute-start | bytes 1179656 | tf_op jit(solution)/shard_map/ppermute | solution.py:390
  53.9 7.3 %shard_map.80 = (bf16[256,1536]{1,0:T(8,128)(2,1)S(1)}, bf16[256,1024]{1,0:T(8,128)(2,1)S(1)}, bf16[256,1536]{1,0:T(8,128)(2,1)S(1)}) custom-call(s32[4]{0:T(128)S(1)} %pad_add_fusion.meta_ref.refs_6_, bf16[768,1536]{1,0:T(8,128)(2,1)S(1)} %copy-done.3, bf16[768,1536]{1,0:T(8,128)(2,1)S(1)} %copy-done.4, bf16[768,1536]{1,0:T(8,128)(2,1)S(1)} %copy-done.5, ...), custom_call_target="tpu_custom_call" | custom-call | flops 1000 | bytes 1000 | tf_op jit(solution)/shard_map/pallas_call | solution.py:173
  63.6 3.6 %shard_map.82 = (bf16[256,768]{1,0:T(8,128)(2,1)S(1)}, bf16[256,768]{1,0:T(8,128)(2,1)S(1)}) custom-call(s32[4]{0:T(128)S(1)} %pad_add_fusion.meta_ref.refs_6_, bf16[256,1536]{1,0:T(8,128)(2,1)S(1)} %get-tuple-element.48.att_hbm, bf16[1536,5120]{1,0:T(8,128)(2,1)S(1)} %copy-done.1, f32[12,40]{1,0:T(8,128)S(1)} %copy-done.6, ...), custom_call_target="tpu_custom_call" | custom-call | flops 1000 | bytes 1000 | tf_op jit(solution)/shard_map/pallas_call | solution.py:238
  67.2 4.5 %collective-permute-done.10.refs_1_ = bf16[256,768]{1,0:T(8,128)(2,1)S(1)} collective-permute-done((bf16[256,768]{1,0:T(8,128)(2,1)S(1)}, bf16[256,768]{1,0:T(8,128)(2,1)S(1)}, u32[]{:S(2)}, u32[]{:S(2)}) %collective-permute-start.10) | collective-permute-done | bytes 393248 | tf_op jit(solution)/shard_map/ppermute | solution.py:390
  72.8 1.6 %collective-permute-start.15 = (bf16[768,256]{1,0:T(8,128)(2,1)S(1)}, bf16[768,256]{1,0:T(8,128)(2,1)S(1)}, u32[]{:S(2)}, u32[]{:S(2)}) collective-permute-start(bf16[768,256]{1,0:T(8,128)(2,1)S(1)} %get-tuple-element.56.refs_4_), channel_id=1, source_target_pairs={{0,4},{4,8},{8,12},{12,0},{1,5},{5,9},{9,13},{13,1},{2,6},{6,10},{... | collective-permute-start | bytes 1179656 | tf_op jit(solution)/shard_map/ppermute | solution.py:405
  74.4 1.5 %collective-permute-start.14 = (bf16[256,768]{1,0:T(8,128)(2,1)S(1)}, bf16[256,768]{1,0:T(8,128)(2,1)S(1)}, u32[]{:S(2)}, u32[]{:S(2)}) collective-permute-start(bf16[256,768]{1,0:T(8,128)(2,1)S(1)} %get-tuple-element.62), channel_id=1, source_target_pairs={{0,2},{1,3},{2,0},{3,1},{4,6},{5,7},{6,4},{7,5},{8,10},{9,11},{10,... | collective-permute-start | bytes 1179656 | tf_op jit(solution)/shard_map/ppermute | solution.py:390
  75.9 9.8 %collective-permute-done.9.refs_3_ = bf16[512,256]{1,0:T(8,128)(2,1)S(1)} collective-permute-done((bf16[512,256]{1,0:T(8,128)(2,1)S(1)}, bf16[512,256]{1,0:T(8,128)(2,1)S(1)}, u32[]{:S(2)}, u32[]{:S(2)}) %collective-permute-start.9) | collective-permute-done | bytes 262176 | tf_op jit(solution)/shard_map/ppermute | solution.py:405
  86.6 2.5 %shard_map.85 = (bf16[256,512]{1,0:T(8,128)(2,1)S(1)}, bf16[256,512]{1,0:T(8,128)(2,1)S(1)}) custom-call(s32[4]{0:T(128)S(1)} %pad_add_fusion.meta_ref.refs_6_, bf16[256,1536]{1,0:T(8,128)(2,1)S(1)} %get-tuple-element.48.att_hbm, bf16[1536,5120]{1,0:T(8,128)(2,1)S(1)} %copy-done.1, f32[12,40]{1,0:T(8,128)S(1)} %copy-done.6, ...), custom_call_target="tpu_custom_call" | custom-call | flops 1000 | bytes 1000 | tf_op jit(solution)/shard_map/pallas_call | solution.py:238
  89.7 1.7 %shard_map.86 = (bf16[768,256]{1,0:T(8,128)(2,1)S(1)}, bf16[1280,768]{1,0:T(8,128)(2,1)}) custom-call(s32[4]{0:T(128)S(1)} %pad_add_fusion.meta_ref.refs_6_, bf16[256,768]{1,0:T(8,128)(2,1)S(1)} %get-tuple-element.55.refs_3_.refs_0_, bf16[256,768]{1,0:T(8,128)(2,1)S(1)} %collective-permute-done.14.refs_1_, ...), custom_call_target="tpu_custom_call", output_to_operand_aliasing={{1}: (6, {})} | custom-call | flops 49999998976 | bytes 1000 | tf_op jit(solution)/shard_map/pallas_call | solution.py:325
  91.4 3.9 %collective-permute-start.17 = (bf16[768,256]{1,0:T(8,128)(2,1)S(1)}, bf16[768,256]{1,0:T(8,128)(2,1)S(1)}, u32[]{:S(2)}, u32[]{:S(2)}) collective-permute-start(bf16[768,256]{1,0:T(8,128)(2,1)S(1)} %get-tuple-element.65.refs_4_), channel_id=1, source_target_pairs={{0,12},{4,0},{8,4},{12,8},{1,13},{5,1},{9,5},{13,9},{2,14},{6,2},{... | collective-permute-start | bytes 1179656 | tf_op jit(solution)/shard_map/ppermute | solution.py:405
  95.2 1.8 %collective-permute-done.12.refs_1_ = bf16[256,512]{1,0:T(8,128)(2,1)S(1)} collective-permute-done((bf16[256,512]{1,0:T(8,128)(2,1)S(1)}, bf16[256,512]{1,0:T(8,128)(2,1)S(1)}, u32[]{:S(2)}, u32[]{:S(2)}) %collective-permute-start.12) | collective-permute-done | bytes 262176 | tf_op jit(solution)/shard_map/ppermute | solution.py:390
  97.3 1.4 %shard_map.87 = (bf16[512,256]{1,0:T(8,128)(2,1)S(1)}, bf16[1280,768]{1,0:T(8,128)(2,1)}) custom-call(s32[4]{0:T(128)S(1)} %pad_add_fusion.meta_ref.refs_6_, bf16[256,512]{1,0:T(8,128)(2,1)S(1)} %get-tuple-element.59.refs_4_.refs_0_, bf16[256,512]{1,0:T(8,128)(2,1)S(1)} %collective-permute-done.12.refs_1_, ...), custom_call_target="tpu_custom_call", output_to_operand_aliasing={{1}: (6, {})} | custom-call | flops 49999998976 | bytes 1000 | tf_op jit(solution)/shard_map/pallas_call | solution.py:325
  98.7 3.4 %collective-permute-start.16 = (bf16[512,256]{1,0:T(8,128)(2,1)S(1)}, bf16[512,256]{1,0:T(8,128)(2,1)S(1)}, u32[]{:S(2)}, u32[]{:S(2)}) collective-permute-start(bf16[512,256]{1,0:T(8,128)(2,1)S(1)} %get-tuple-element.67.refs_1_), channel_id=1, source_target_pairs={{0,12},{4,0},{8,4},{12,8},{1,13},{5,1},{9,5},{13,9},{2,14},{6,2},{... | collective-permute-start | bytes 786440 | tf_op jit(solution)/shard_map/ppermute | solution.py:405
  102.1 2.8 %collective-permute-done.17.refs_0_ = bf16[768,256]{1,0:T(8,128)(2,1)S(1)} collective-permute-done((bf16[768,256]{1,0:T(8,128)(2,1)S(1)}, bf16[768,256]{1,0:T(8,128)(2,1)S(1)}, u32[]{:S(2)}, u32[]{:S(2)}) %collective-permute-start.17) | collective-permute-done | bytes 393248 | tf_op jit(solution)/shard_map/ppermute | solution.py:405
  104.9 1.3 %shard_map.88.refs_1_ = bf16[1280,768]{1,0:T(8,128)(2,1)} custom-call(s32[4]{0:T(128)S(1)} %pad_add_fusion.meta_ref.refs_6_, bf16[768,256]{1,0:T(8,128)(2,1)S(1)} %collective-permute-done.17.refs_0_, bf16[512,256]{1,0:T(8,128)(2,1)S(1)} %get-tuple-element.67.refs_1_, bf16[1280,768]{1,0:T(8,128)(2,1)} %get-tuple-element.68.refs_2_), custom_call_target="tpu_custom_call", output_to_operand_aliasing={{}: (3, {})} | custom-call | flops 1000 | bytes 1000 | tf_op jit(solution)/shard_map/pallas_call | solution.py:325
  106.2 4.2 %collective-permute-done.16.refs_0_ = bf16[512,256]{1,0:T(8,128)(2,1)S(1)} collective-permute-done((bf16[512,256]{1,0:T(8,128)(2,1)S(1)}, bf16[512,256]{1,0:T(8,128)(2,1)S(1)}, u32[]{:S(2)}, u32[]{:S(2)}) %collective-permute-start.16) | collective-permute-done | bytes 262176 | tf_op jit(solution)/shard_map/ppermute | solution.py:405
  110.4 1.3 %shard_map.89 = bf16[1280,768]{1,0:T(8,128)(2,1)} custom-call(s32[4]{0:T(128)S(1)} %pad_add_fusion.meta_ref.refs_6_, bf16[512,256]{1,0:T(8,128)(2,1)S(1)} %collective-permute-done.16.refs_0_, bf16[1280,768]{1,0:T(8,128)(2,1)} %shard_map.88.refs_1_), custom_call_target="tpu_custom_call", output_to_operand_aliasing={{}: (2, {})} | custom-call | flops 1000 | bytes 1000 | tf_op jit(solution)/shard_map/pallas_call | solution.py:325
  (37 shorter events, 9.8 us)
Async XLA Ops:
  1.4 5.5 %copy-start = (bf16[1536,5120]{1,0:T(8,128)(2,1)S(1)}, bf16[1536,5120]{1,0:T(8,128)(2,1)}, u32[]{:S(2)}) copy-start(bf16[1536,5120]{1,0:T(8,128)(2,1)} %w_hbm.11) | copy-start | bytes 47185924
  6.9 1.7 %copy-start.2 = (bf16[768,1536]{1,0:T(8,128)(2,1)S(1)}, bf16[768,1536]{1,0:T(8,128)(2,1)}, u32[]{:S(2)}) copy-start(bf16[768,1536]{1,0:T(8,128)(2,1)} %refs_0_.5) | copy-start | bytes 7077892
  8.6 1.7 %copy-start.4 = (bf16[768,1536]{1,0:T(8,128)(2,1)S(1)}, bf16[768,1536]{1,0:T(8,128)(2,1)}, u32[]{:S(2)}) copy-start(bf16[768,1536]{1,0:T(8,128)(2,1)} %refs_1_.5) | copy-start | bytes 7077892
  10.2 1.7 %copy-start.5 = (bf16[768,1536]{1,0:T(8,128)(2,1)S(1)}, bf16[768,1536]{1,0:T(8,128)(2,1)}, u32[]{:S(2)}) copy-start(bf16[768,1536]{1,0:T(8,128)(2,1)} %refs_2_.5) | copy-start | bytes 7077892
  11.9 0.7 copy-start.6
  12.6 9.7 %copy-start.1 = (bf16[1536,5120]{1,0:T(8,128)(2,1)S(1)}, bf16[1536,5120]{1,0:T(8,128)(2,1)}, u32[]{:S(2)}) copy-start(bf16[1536,5120]{1,0:T(8,128)(2,1)} %w_hbm.11) | copy-start | bytes 47185924
  19.9 2.4 %collective-permute-start.1 = (bf16[256,1536]{1,0:T(8,128)(2,1)S(1)}, bf16[256,1536]{1,0:T(8,128)(2,1)S(1)}, u32[]{:S(2)}, u32[]{:S(2)}) collective-permute-start(bf16[256,1536]{1,0:T(8,128)(2,1)S(1)} %get-tuple-element.39.refs_1_), channel_id=1, source_target_pairs={{0,1},{1,0},{2,3},{3,2},{4,5},{5,4},{6,7},{7,6},{8,9},{9,8},{10,11... | collective-permute-start | bytes 2359304 | tf_op jit(solution)/shard_map/ppermute | solution.py:382
  25.7 12.3 %collective-permute-start.4 = (bf16[256,768]{1,0:T(8,128)(2,1)S(1)}, bf16[256,768]{1,0:T(8,128)(2,1)S(1)}, u32[]{:S(2)}, u32[]{:S(2)}) collective-permute-start(bf16[256,768]{1,0:T(8,128)(2,1)S(1)} %get-tuple-element.44), channel_id=1, source_target_pairs={{0,2},{1,3},{2,0},{3,1},{4,6},{5,7},{6,4},{7,5},{8,10},{9,11},{10,... | collective-permute-start | bytes 1179656 | tf_op jit(solution)/shard_map/ppermute | solution.py:390
  28.6 19.2 %collective-permute-start = (bf16[256,1024]{1,0:T(8,128)(2,1)S(1)}, bf16[256,1024]{1,0:T(8,128)(2,1)S(1)}, u32[]{:S(2)}, u32[]{:S(2)}) collective-permute-start(bf16[256,1024]{1,0:T(8,128)(2,1)S(1)} %get-tuple-element.38), channel_id=1, source_target_pairs={{0,1},{1,0},{2,3},{3,2},{4,5},{5,4},{6,7},{7,6},{8,9},{9,8},{10,11... | collective-permute-start | bytes 1572872 | tf_op jit(solution)/shard_map/ppermute | solution.py:382
  36.1 5.8 %collective-permute-start.3 = (bf16[256,1024]{1,0:T(8,128)(2,1)S(1)}, bf16[256,1024]{1,0:T(8,128)(2,1)S(1)}, u32[]{:S(2)}, u32[]{:S(2)}) collective-permute-start(bf16[256,1024]{1,0:T(8,128)(2,1)S(1)} %get-tuple-element.43), channel_id=1, source_target_pairs={{0,1},{1,0},{2,3},{3,2},{4,5},{5,4},{6,7},{7,6},{8,9},{9,8},{10,11... | collective-permute-start | bytes 1572872 | tf_op jit(solution)/shard_map/ppermute | solution.py:382
  36.7 7.7 %collective-permute-start.2 = (bf16[256,1536]{1,0:T(8,128)(2,1)S(1)}, bf16[256,1536]{1,0:T(8,128)(2,1)S(1)}, u32[]{:S(2)}, u32[]{:S(2)}) collective-permute-start(bf16[256,1536]{1,0:T(8,128)(2,1)S(1)} %get-tuple-element.42.refs_2_), channel_id=1, source_target_pairs={{0,1},{1,0},{2,3},{3,2},{4,5},{5,4},{6,7},{7,6},{8,9},{9,8},{10,11... | collective-permute-start | bytes 2359304 | tf_op jit(solution)/shard_map/ppermute | solution.py:382
  39.0 22.3 %collective-permute-start.8 = (bf16[768,256]{1,0:T(8,128)(2,1)S(1)}, bf16[768,256]{1,0:T(8,128)(2,1)S(1)}, u32[]{:S(2)}, u32[]{:S(2)}) collective-permute-start(bf16[768,256]{1,0:T(8,128)(2,1)S(1)} %shard_map.76.refs_1_.refs_2_), channel_id=1, source_target_pairs={{0,8},{4,12},{8,0},{12,4},{1,9},{5,13},{9,1},{13,5},{2,10},{6,14},... | collective-permute-start | bytes 1179656 | tf_op jit(solution)/shard_map/ppermute | solution.py:405
  47.8 6.1 %copy-start.3 = (bf16[768,1536]{1,0:T(8,128)(2,1)S(1)}, bf16[768,1536]{1,0:T(8,128)(2,1)}, u32[]{:S(2)}) copy-start(bf16[768,1536]{1,0:T(8,128)(2,1)} %refs_0_.5) | copy-start | bytes 7077892
  50.4 10.9 %collective-permute-start.7 = (bf16[256,512]{1,0:T(8,128)(2,1)S(1)}, bf16[256,512]{1,0:T(8,128)(2,1)S(1)}, u32[]{:S(2)}, u32[]{:S(2)}) collective-permute-start(bf16[256,512]{1,0:T(8,128)(2,1)S(1)} %get-tuple-element.51), channel_id=1, source_target_pairs={{0,2},{1,3},{2,0},{3,1},{4,6},{5,7},{6,4},{7,5},{8,10},{9,11},{10,... | collective-permute-start | bytes 786440 | tf_op jit(solution)/shard_map/ppermute | solution.py:390
  51.9 24.0 %collective-permute-start.6 = (bf16[256,512]{1,0:T(8,128)(2,1)S(1)}, bf16[256,512]{1,0:T(8,128)(2,1)S(1)}, u32[]{:S(2)}, u32[]{:S(2)}) collective-permute-start(bf16[256,512]{1,0:T(8,128)(2,1)S(1)} %get-tuple-element.50), channel_id=1, source_target_pairs={{0,2},{1,3},{2,0},{3,1},{4,6},{5,7},{6,4},{7,5},{8,10},{9,11},{10,... | collective-permute-start | bytes 786440 | tf_op jit(solution)/shard_map/ppermute | solution.py:390
  52.4 19.2 %collective-permute-start.10 = (bf16[256,768]{1,0:T(8,128)(2,1)S(1)}, bf16[256,768]{1,0:T(8,128)(2,1)S(1)}, u32[]{:S(2)}, u32[]{:S(2)}) collective-permute-start(bf16[256,768]{1,0:T(8,128)(2,1)S(1)} %get-tuple-element.54), channel_id=1, source_target_pairs={{0,2},{1,3},{2,0},{3,1},{4,6},{5,7},{6,4},{7,5},{8,10},{9,11},{10,... | collective-permute-start | bytes 1179656 | tf_op jit(solution)/shard_map/ppermute | solution.py:390
  61.2 2.4 %collective-permute-start.11 = (bf16[256,1536]{1,0:T(8,128)(2,1)S(1)}, bf16[256,1536]{1,0:T(8,128)(2,1)S(1)}, u32[]{:S(2)}, u32[]{:S(2)}) collective-permute-start(bf16[256,1536]{1,0:T(8,128)(2,1)S(1)} %get-tuple-element.52.refs_3_), channel_id=1, source_target_pairs={{0,1},{1,0},{2,3},{3,2},{4,5},{5,4},{6,7},{7,6},{8,9},{9,8},{10,11... | collective-permute-start | bytes 2359304 | tf_op jit(solution)/shard_map/ppermute | solution.py:382
  62.0 23.7 %collective-permute-start.9 = (bf16[512,256]{1,0:T(8,128)(2,1)S(1)}, bf16[512,256]{1,0:T(8,128)(2,1)S(1)}, u32[]{:S(2)}, u32[]{:S(2)}) collective-permute-start(bf16[512,256]{1,0:T(8,128)(2,1)S(1)} %get-tuple-element.53.refs_1_.refs_2_), channel_id=1, source_target_pairs={{0,8},{4,12},{8,0},{12,4},{1,9},{5,13},{9,1},{13,5},{2,10},{6,14},... | collective-permute-start | bytes 786440 | tf_op jit(solution)/shard_map/ppermute | solution.py:405
  62.5 24.1 %collective-permute-start.5 = (bf16[256,1024]{1,0:T(8,128)(2,1)S(1)}, bf16[256,1024]{1,0:T(8,128)(2,1)S(1)}, u32[]{:S(2)}, u32[]{:S(2)}) collective-permute-start(bf16[256,1024]{1,0:T(8,128)(2,1)S(1)} %get-tuple-element.49), channel_id=1, source_target_pairs={{0,1},{1,0},{2,3},{3,2},{4,5},{5,4},{6,7},{7,6},{8,9},{9,8},{10,11... | collective-permute-start | bytes 1572872 | tf_op jit(solution)/shard_map/ppermute | solution.py:382
  72.8 16.9 %collective-permute-start.15 = (bf16[768,256]{1,0:T(8,128)(2,1)S(1)}, bf16[768,256]{1,0:T(8,128)(2,1)S(1)}, u32[]{:S(2)}, u32[]{:S(2)}) collective-permute-start(bf16[768,256]{1,0:T(8,128)(2,1)S(1)} %get-tuple-element.56.refs_4_), channel_id=1, source_target_pairs={{0,4},{4,8},{8,12},{12,0},{1,5},{5,9},{9,13},{13,1},{2,6},{6,10},{... | collective-permute-start | bytes 1179656 | tf_op jit(solution)/shard_map/ppermute | solution.py:405
  74.4 15.3 %collective-permute-start.14 = (bf16[256,768]{1,0:T(8,128)(2,1)S(1)}, bf16[256,768]{1,0:T(8,128)(2,1)S(1)}, u32[]{:S(2)}, u32[]{:S(2)}) collective-permute-start(bf16[256,768]{1,0:T(8,128)(2,1)S(1)} %get-tuple-element.62), channel_id=1, source_target_pairs={{0,2},{1,3},{2,0},{3,1},{4,6},{5,7},{6,4},{7,5},{8,10},{9,11},{10,... | collective-permute-start | bytes 1179656 | tf_op jit(solution)/shard_map/ppermute | solution.py:390
  86.5 10.8 %collective-permute-start.13 = (bf16[512,256]{1,0:T(8,128)(2,1)S(1)}, bf16[512,256]{1,0:T(8,128)(2,1)S(1)}, u32[]{:S(2)}, u32[]{:S(2)}) collective-permute-start(bf16[512,256]{1,0:T(8,128)(2,1)S(1)} %get-tuple-element.58.refs_1_), channel_id=1, source_target_pairs={{0,4},{4,8},{8,12},{12,0},{1,5},{5,9},{9,13},{13,1},{2,6},{6,10},{... | collective-permute-start | bytes 786440 | tf_op jit(solution)/shard_map/ppermute | solution.py:405
  89.1 8.0 %collective-permute-start.12 = (bf16[256,512]{1,0:T(8,128)(2,1)S(1)}, bf16[256,512]{1,0:T(8,128)(2,1)S(1)}, u32[]{:S(2)}, u32[]{:S(2)}) collective-permute-start(bf16[256,512]{1,0:T(8,128)(2,1)S(1)} %get-tuple-element.60), channel_id=1, source_target_pairs={{0,2},{1,3},{2,0},{3,1},{4,6},{5,7},{6,4},{7,5},{8,10},{9,11},{10,... | collective-permute-start | bytes 786440 | tf_op jit(solution)/shard_map/ppermute | solution.py:390
  91.4 13.5 %collective-permute-start.17 = (bf16[768,256]{1,0:T(8,128)(2,1)S(1)}, bf16[768,256]{1,0:T(8,128)(2,1)S(1)}, u32[]{:S(2)}, u32[]{:S(2)}) collective-permute-start(bf16[768,256]{1,0:T(8,128)(2,1)S(1)} %get-tuple-element.65.refs_4_), channel_id=1, source_target_pairs={{0,12},{4,0},{8,4},{12,8},{1,13},{5,1},{9,5},{13,9},{2,14},{6,2},{... | collective-permute-start | bytes 1179656 | tf_op jit(solution)/shard_map/ppermute | solution.py:405
  98.7 11.7 %collective-permute-start.16 = (bf16[512,256]{1,0:T(8,128)(2,1)S(1)}, bf16[512,256]{1,0:T(8,128)(2,1)S(1)}, u32[]{:S(2)}, u32[]{:S(2)}) collective-permute-start(bf16[512,256]{1,0:T(8,128)(2,1)S(1)} %get-tuple-element.67.refs_1_), channel_id=1, source_target_pairs={{0,12},{4,0},{8,4},{12,8},{1,13},{5,1},{9,5},{13,9},{2,14},{6,2},{... | collective-permute-start | bytes 786440 | tf_op jit(solution)/shard_map/ppermute | solution.py:405
where the time goes:
time: 112 us
  Pallas kernels  49.1 us (44%)
  waiting for transfers between devices  27.5 us (25%)
  starting transfers between devices  22.3 us (20%)
  local copies, waits for them, and re-layouts  11.9 us (11%)
    pallas_call x3, Pallas kernels, sibling_part(): pl.pallas_call(functools.partial(sibling_kernel, features, slot, ranges,...  22 us
    pallas_call x6, Pallas kernels, own_part(): pl.pallas_call(functools.partial(own_kernel, features, chunk, len(receive...  17.9 us
    ppermute x6, waiting for transfers between devices, pipeline(): lax.ppermute(token, 'dp', [(i, (i + SHIFTS[slot]) % groups) for i in rang...  17 us
    ppermute x6, starting transfers between devices, pipeline(): lax.ppermute(token, 'dp', [(i, (i + SHIFTS[slot]) % groups) for i in rang...  12.2 us
    unnamed x14, local copies, waits for them, and re-layouts  11.2 us
    pallas_call x8, Pallas kernels, finish(): pl.pallas_call(functools.partial(finish_kernel, slot, first, into, [a[:2]...  9.18 us
    ppermute x6, starting transfers between devices, pipeline(): from_chip[index] = lax.ppermute(send, 'tensor', other_chip)  8.61 us
    ppermute x6, waiting for transfers between devices, pipeline(): from_chip[index] = lax.ppermute(send, 'tensor', other_chip)  7.67 us
  transfers between devices with their start and end apart: 18, of which 9 were waited for; matrix products, arithmetic and copies ran while one was open for 0% of the time, Pallas kernels for 33%

commit v1 on v0

--- a/solution.py
+++ b/solution.py
@@ -12,7 +12,7 @@
 WIDE = 256
 NEG = -1e30
 LOG2E = 1.4426950408889634
-VMEM = 16 * 1024 * 1024
+VMEM = 50 * 1024 * 1024
 HEADS_STEP = 4
 
 ANY = pl.BlockSpec(memory_space=pl.ANY)
@@ -345,15 +345,15 @@
 SHORT = pl.CostEstimate(flops=1000, bytes_accessed=1000, transcendentals=0)
 LONG = pl.CostEstimate(flops=5 * 10**10, bytes_accessed=1000, transcendentals=0)
 
-SHIFTS = (2, 1, 3)
+SHIFTS = (2, 3, 1)
 CHUNKS = ((0, 0, 768), (0, 768, 512), (1, 0, 768), (1, 768, 512), (2, 0, 768), (2, 768, 512))
 SHARES = ((0, (0, 1)), (1, (2, 3)), (2, (4, 5)))
 CUT = None
 STEPS = (
-    "s0", "o0", "s1", "f0", "o3", "o2", "p0", "o1", "s2", "f1", "o4", "f2", "p1", "f3", "p2", "o5", "f4",
-    "p3", "f5", "p4", "p5",
+    "s0", "o1", "o0", "f1", "s1", "p1", "s2", "f0", "o4", "p0", "o3", "o2", "f3", "o5", "f2", "p3", "f4",
+    "p2", "f5", "p4", "p5",
 )
-COUNT_LONG = ("f0", "f1", "f3", "f4", "f5",)
+COUNT_LONG = ("f0", "f1", "f3", "f4", "o0", "o1", "o4", "s0",)
 
 
 def pipeline(meta, queries, keys, values, segment, w_out, w_scale):

time: 112 us -> 105 us (0.938)
  local copies, waits for them, and re-layouts: 11.9 us -> 1.39 us
  Pallas kernels: 49.1 us -> 56.7 us
  waiting for transfers between devices: 27.5 us -> 24.3 us
  starting transfers between devices: 22.3 us -> 20.8 us
    unnamed x14 -> x4, local copies, waits for them, and re-layouts: 11.2 us -> 0.7 us
    pallas_call x6, Pallas kernels: 17.9 us -> 22.9 us  [own_part(): pl.pallas_call(functools.partial(own_kernel, features, chunk, len(receive...]
    ppermute x6, waiting for transfers between devices: 17 us -> 12.4 us  [pipeline(): lax.ppermute(token, 'dp', [(i, (i + SHIFTS[slot]) % groups) for i in rang...]
    ppermute x6, starting transfers between devices: 12.2 us -> 9.39 us  [pipeline(): lax.ppermute(token, 'dp', [(i, (i + SHIFTS[slot]) % groups) for i in rang...]
    pallas_call x3, Pallas kernels: 22 us -> 24.6 us  [sibling_part(): pl.pallas_call(functools.partial(sibling_kernel, features, slot, ranges,...]
    ppermute x6, waiting for transfers between devices: 7.67 us -> 9.06 us  [pipeline(): from_chip[index] = lax.ppermute(send, 'tensor', other_chip)]
    ppermute x6, starting transfers between devices: 8.61 us -> 9.95 us  [pipeline(): from_chip[index] = lax.ppermute(send, 'tensor', other_chip)]
  transfers between devices with their start and end apart: 18 -> 18, of which waited for: 9 -> 8; matrix products, arithmetic and copies ran while one was open for 0% -> 0% of each run, Pallas kernels for 33% -> 45%
where the time goes in v1:
time: 105 us; the launch traced here: 104 us
  Pallas kernels  56.7 us (54%)
  waiting for transfers between devices  24.3 us (23%)
  starting transfers between devices  20.8 us (20%)
  local copies, waits for them, and re-layouts  1.39 us (1%)
    pallas_call x3, Pallas kernels, sibling_part(): pl.pallas_call(functools.partial(sibling_kernel, features, slot, ranges,...  24.6 us
    pallas_call x6, Pallas kernels, own_part(): pl.pallas_call(functools.partial(own_kernel, features, chunk, len(receive...  22.9 us
    ppermute x6, waiting for transfers between devices, pipeline(): lax.ppermute(token, 'dp', [(i, (i + SHIFTS[slot]) % groups) for i in rang...  12.4 us
    ppermute x6, starting transfers between devices, pipeline(): from_chip[index] = lax.ppermute(send, 'tensor', other_chip)  9.95 us
    ppermute x6, starting transfers between devices, pipeline(): lax.ppermute(token, 'dp', [(i, (i + SHIFTS[slot]) % groups) for i in rang...  9.39 us
    pallas_call x8, Pallas kernels, finish(): pl.pallas_call(functools.partial(finish_kernel, slot, first, into, [a[:2]...  9.19 us
    ppermute x6, waiting for transfers between devices, pipeline(): from_chip[index] = lax.ppermute(send, 'tensor', other_chip)  9.06 us
    ppermute x6, waiting for transfers between devices, pipeline(): lax.ppermute(array, 'tensor', other_core)  2.85 us
  transfers between devices with their start and end apart: 18, of which 8 were waited for; matrix products, arithmetic and copies ran while one was open for 0% of the time, Pallas kernels for 45%

profile of v1, /device:TPU:0, one launch (start us, length us, event | category | flops | bytes accessed | tf_op | source)
XLA Modules:
  0.0 104.3 jit_solution(10958130220937641904)
XLA Ops:
  2.1 8.1 %shard_map.73 = (bf16[256,1536]{1,0:T(8,128)(2,1)S(1)}, bf16[256,1024]{1,0:T(8,128)(2,1)S(1)}, bf16[256,1536]{1,0:T(8,128)(2,1)S(1)}) custom-call(s32[4]{0:T(128)S(1)} %pad_add_fusion.meta_ref.refs_6_, bf16[768,1536]{1,0:T(8,128)(2,1)} %refs_0_.5, bf16[768,1536]{1,0:T(8,128)(2,1)} %refs_1_.5, bf16[768,1536]{1,0:T(8,128)(2,1)} %refs_2_.5, ...), custom_call_target="tpu_custom_call" | custom-call | flops 49999998976 | bytes 1000 | tf_op jit(solution)/shard_map/pallas_call | solution.py:173
  11.0 1.5 %collective-permute-done.refs_0_ = bf16[256,1024]{1,0:T(8,128)(2,1)S(1)} collective-permute-done((bf16[256,1024]{1,0:T(8,128)(2,1)S(1)}, bf16[256,1024]{1,0:T(8,128)(2,1)S(1)}, u32[]{:S(2)}, u32[]{:S(2)}) %collective-permute-start) | collective-permute-done | bytes 524320 | tf_op jit(solution)/shard_map/ppermute | solution.py:382
  12.4 3.3 %shard_map.74 = (bf16[256,512]{1,0:T(8,128)(2,1)S(1)}, bf16[256,512]{1,0:T(8,128)(2,1)S(1)}) custom-call(s32[4]{0:T(128)S(1)} %pad_add_fusion.meta_ref.refs_6_, bf16[256,1536]{1,0:T(8,128)(2,1)S(1)} %get-tuple-element.37.att_hbm, bf16[1536,5120]{1,0:T(8,128)(2,1)} %w_hbm.11, f32[12,40]{1,0:T(8,128)S(1)} %copy-done.1, ...), custom_call_target="tpu_custom_call" | custom-call | flops 49999998976 | bytes 1000 | tf_op jit(solution)/shard_map/pallas_call | solution.py:238
  15.7 2.9 %collective-permute-start.1 = (bf16[256,512]{1,0:T(8,128)(2,1)S(1)}, bf16[256,512]{1,0:T(8,128)(2,1)S(1)}, u32[]{:S(2)}, u32[]{:S(2)}) collective-permute-start(bf16[256,512]{1,0:T(8,128)(2,1)S(1)} %get-tuple-element.41), channel_id=1, source_target_pairs={{0,2},{1,3},{2,0},{3,1},{4,6},{5,7},{6,4},{7,5},{8,10},{9,11},{10,... | collective-permute-start | bytes 786440 | tf_op jit(solution)/shard_map/ppermute | solution.py:390
  18.6 4.3 %shard_map.75 = (bf16[256,768]{1,0:T(8,128)(2,1)S(1)}, bf16[256,768]{1,0:T(8,128)(2,1)S(1)}) custom-call(s32[4]{0:T(128)S(1)} %pad_add_fusion.meta_ref.refs_6_, bf16[256,1536]{1,0:T(8,128)(2,1)S(1)} %get-tuple-element.37.att_hbm, bf16[1536,5120]{1,0:T(8,128)(2,1)} %w_hbm.11, f32[12,40]{1,0:T(8,128)S(1)} %copy-done.1, ...), custom_call_target="tpu_custom_call" | custom-call | flops 49999998976 | bytes 1000 | tf_op jit(solution)/shard_map/pallas_call | solution.py:238
  23.1 2.2 %collective-permute-done.1.refs_1_ = bf16[256,512]{1,0:T(8,128)(2,1)S(1)} collective-permute-done((bf16[256,512]{1,0:T(8,128)(2,1)S(1)}, bf16[256,512]{1,0:T(8,128)(2,1)S(1)}, u32[]{:S(2)}, u32[]{:S(2)}) %collective-permute-start.1) | collective-permute-done | bytes 262176 | tf_op jit(solution)/shard_map/ppermute | solution.py:390
  26.0 2.8 %collective-permute-start.7 = (bf16[512,256]{1,0:T(8,128)(2,1)S(1)}, bf16[512,256]{1,0:T(8,128)(2,1)S(1)}, u32[]{:S(2)}, u32[]{:S(2)}) collective-permute-start(bf16[512,256]{1,0:T(8,128)(2,1)S(1)} %shard_map.76.refs_6_.refs_2_), channel_id=1, source_target_pairs={{0,8},{4,12},{8,0},{12,4},{1,9},{5,13},{9,1},{13,5},{2,10},{6,14},... | collective-permute-start | bytes 786440 | tf_op jit(solution)/shard_map/ppermute | solution.py:405
  28.8 8.3 %shard_map.77 = (bf16[256,1536]{1,0:T(8,128)(2,1)S(1)}, bf16[256,1024]{1,0:T(8,128)(2,1)S(1)}, bf16[256,1536]{1,0:T(8,128)(2,1)S(1)}) custom-call(s32[4]{0:T(128)S(1)} %pad_add_fusion.meta_ref.refs_6_, bf16[768,1536]{1,0:T(8,128)(2,1)} %refs_0_.5, bf16[768,1536]{1,0:T(8,128)(2,1)} %refs_1_.5, bf16[768,1536]{1,0:T(8,128)(2,1)} %refs_2_.5, ...), custom_call_target="tpu_custom_call" | custom-call | flops 1000 | bytes 1000 | tf_op jit(solution)/shard_map/pallas_call | solution.py:173
  37.2 8.1 %shard_map.78 = (bf16[256,1536]{1,0:T(8,128)(2,1)S(1)}, bf16[256,1024]{1,0:T(8,128)(2,1)S(1)}, bf16[256,1536]{1,0:T(8,128)(2,1)S(1)}) custom-call(s32[4]{0:T(128)S(1)} %pad_add_fusion.meta_ref.refs_6_, bf16[768,1536]{1,0:T(8,128)(2,1)} %refs_0_.5, bf16[768,1536]{1,0:T(8,128)(2,1)} %refs_1_.5, bf16[768,1536]{1,0:T(8,128)(2,1)} %refs_2_.5, ...), custom_call_target="tpu_custom_call" | custom-call | flops 1000 | bytes 1000 | tf_op jit(solution)/shard_map/pallas_call | solution.py:173
  46.0 0.9 shard_map.79
  47.2 1.4 %collective-permute-done.5.refs_0_ = bf16[256,1536]{1,0:T(8,128)(2,1)S(1)} collective-permute-done((bf16[256,1536]{1,0:T(8,128)(2,1)S(1)}, bf16[256,1536]{1,0:T(8,128)(2,1)S(1)}, u32[]{:S(2)}, u32[]{:S(2)}) %collective-permute-start.5) | collective-permute-done | bytes 786464 | tf_op jit(solution)/shard_map/ppermute | solution.py:382
  48.6 4.3 %shard_map.80 = (bf16[256,768]{1,0:T(8,128)(2,1)S(1)}, bf16[256,768]{1,0:T(8,128)(2,1)S(1)}) custom-call(s32[4]{0:T(128)S(1)} %pad_add_fusion.meta_ref.refs_6_, bf16[256,1536]{1,0:T(8,128)(2,1)S(1)} %get-tuple-element.44.att_hbm, bf16[1536,5120]{1,0:T(8,128)(2,1)} %w_hbm.11, f32[12,40]{1,0:T(8,128)S(1)} %copy-done.1, ...), custom_call_target="tpu_custom_call" | custom-call | flops 49999998976 | bytes 1000 | tf_op jit(solution)/shard_map/pallas_call | solution.py:238
  52.9 3.3 %shard_map.81 = (bf16[256,512]{1,0:T(8,128)(2,1)S(1)}, bf16[256,512]{1,0:T(8,128)(2,1)S(1)}) custom-call(s32[4]{0:T(128)S(1)} %pad_add_fusion.meta_ref.refs_6_, bf16[256,1536]{1,0:T(8,128)(2,1)S(1)} %get-tuple-element.46.att_hbm, bf16[1536,5120]{1,0:T(8,128)(2,1)} %w_hbm.11, f32[12,40]{1,0:T(8,128)S(1)} %copy-done.1, ...), custom_call_target="tpu_custom_call" | custom-call | flops 1000 | bytes 1000 | tf_op jit(solution)/shard_map/pallas_call | solution.py:238
  56.2 2.4 %collective-permute-start.8 = (bf16[256,512]{1,0:T(8,128)(2,1)S(1)}, bf16[256,512]{1,0:T(8,128)(2,1)S(1)}, u32[]{:S(2)}, u32[]{:S(2)}) collective-permute-start(bf16[256,512]{1,0:T(8,128)(2,1)S(1)} %get-tuple-element.53), channel_id=1, source_target_pairs={{0,2},{1,3},{2,0},{3,1},{4,6},{5,7},{6,4},{7,5},{8,10},{9,11},{10,... | collective-permute-start | bytes 786440 | tf_op jit(solution)/shard_map/ppermute | solution.py:390
  58.7 4.3 %shard_map.82 = (bf16[256,768]{1,0:T(8,128)(2,1)S(1)}, bf16[256,768]{1,0:T(8,128)(2,1)S(1)}) custom-call(s32[4]{0:T(128)S(1)} %pad_add_fusion.meta_ref.refs_6_, bf16[256,1536]{1,0:T(8,128)(2,1)S(1)} %get-tuple-element.46.att_hbm, bf16[1536,5120]{1,0:T(8,128)(2,1)} %w_hbm.11, f32[12,40]{1,0:T(8,128)S(1)} %copy-done.1, ...), custom_call_target="tpu_custom_call" | custom-call | flops 1000 | bytes 1000 | tf_op jit(solution)/shard_map/pallas_call | solution.py:238
  63.5 1.7 %collective-permute-start.14 = (bf16[256,768]{1,0:T(8,128)(2,1)S(1)}, bf16[256,768]{1,0:T(8,128)(2,1)S(1)}, u32[]{:S(2)}, u32[]{:S(2)}) collective-permute-start(bf16[256,768]{1,0:T(8,128)(2,1)S(1)} %get-tuple-element.62), channel_id=1, source_target_pairs={{0,2},{1,3},{2,0},{3,1},{4,6},{5,7},{6,4},{7,5},{8,10},{9,11},{10,... | collective-permute-start | bytes 1179656 | tf_op jit(solution)/shard_map/ppermute | solution.py:390
  65.2 2.6 %collective-permute-done.9.refs_3_ = bf16[768,256]{1,0:T(8,128)(2,1)S(1)} collective-permute-done((bf16[768,256]{1,0:T(8,128)(2,1)S(1)}, bf16[768,256]{1,0:T(8,128)(2,1)S(1)}, u32[]{:S(2)}, u32[]{:S(2)}) %collective-permute-start.9) | collective-permute-done | bytes 393248 | tf_op jit(solution)/shard_map/ppermute | solution.py:405
  68.5 1.2 %collective-permute-start.15 = (bf16[512,256]{1,0:T(8,128)(2,1)S(1)}, bf16[512,256]{1,0:T(8,128)(2,1)S(1)}, u32[]{:S(2)}, u32[]{:S(2)}) collective-permute-start(bf16[512,256]{1,0:T(8,128)(2,1)S(1)} %get-tuple-element.56.refs_1_), channel_id=1, source_target_pairs={{0,12},{4,0},{8,4},{12,8},{1,13},{5,1},{9,5},{13,9},{2,14},{6,2},{... | collective-permute-start | bytes 786440 | tf_op jit(solution)/shard_map/ppermute | solution.py:405
  69.8 3.3 %shard_map.84 = (bf16[256,512]{1,0:T(8,128)(2,1)S(1)}, bf16[256,512]{1,0:T(8,128)(2,1)S(1)}) custom-call(s32[4]{0:T(128)S(1)} %pad_add_fusion.meta_ref.refs_6_, bf16[256,1536]{1,0:T(8,128)(2,1)S(1)} %get-tuple-element.44.att_hbm, bf16[1536,5120]{1,0:T(8,128)(2,1)} %w_hbm.11, f32[12,40]{1,0:T(8,128)S(1)} %copy-done.1, ...), custom_call_target="tpu_custom_call" | custom-call | flops 1000 | bytes 1000 | tf_op jit(solution)/shard_map/pallas_call | solution.py:238
  73.1 2.5 %collective-permute-start.11 = (bf16[256,512]{1,0:T(8,128)(2,1)S(1)}, bf16[256,512]{1,0:T(8,128)(2,1)S(1)}, u32[]{:S(2)}, u32[]{:S(2)}) collective-permute-start(bf16[256,512]{1,0:T(8,128)(2,1)S(1)} %get-tuple-element.58), channel_id=1, source_target_pairs={{0,2},{1,3},{2,0},{3,1},{4,6},{5,7},{6,4},{7,5},{8,10},{9,11},{10,... | collective-permute-start | bytes 786440 | tf_op jit(solution)/shard_map/ppermute | solution.py:390
  75.5 1.1 %shard_map.85 = (bf16[768,256]{1,0:T(8,128)(2,1)S(1)}, bf16[768,256]{1,0:T(8,128)(2,1)S(1)}) custom-call(s32[4]{0:T(128)S(1)} %pad_add_fusion.meta_ref.refs_6_, bf16[256,768]{1,0:T(8,128)(2,1)S(1)} %get-tuple-element.54.refs_4_.refs_0_, bf16[256,768]{1,0:T(8,128)(2,1)S(1)} %collective-permute-done.12.refs_1_, ...), custom_call_target="tpu_custom_call" | custom-call | flops 1000 | bytes 1000 | tf_op jit(solution)/shard_map/pallas_call | solution.py:325
  76.7 1.9 %collective-permute-start.13 = (bf16[768,256]{1,0:T(8,128)(2,1)S(1)}, bf16[768,256]{1,0:T(8,128)(2,1)S(1)}, u32[]{:S(2)}, u32[]{:S(2)}) collective-permute-start(bf16[768,256]{1,0:T(8,128)(2,1)S(1)} %get-tuple-element.61.refs_4_), channel_id=1, source_target_pairs={{0,12},{4,0},{8,4},{12,8},{1,13},{5,1},{9,5},{13,9},{2,14},{6,2},{... | collective-permute-start | bytes 1179656 | tf_op jit(solution)/shard_map/ppermute | solution.py:405
  78.5 5.0 %collective-permute-done.14.refs_1_ = bf16[256,768]{1,0:T(8,128)(2,1)S(1)} collective-permute-done((bf16[256,768]{1,0:T(8,128)(2,1)S(1)}, bf16[256,768]{1,0:T(8,128)(2,1)S(1)}, u32[]{:S(2)}, u32[]{:S(2)}) %collective-permute-start.14) | collective-permute-done | bytes 393248 | tf_op jit(solution)/shard_map/ppermute | solution.py:390
  83.5 1.7 %shard_map.86 = (bf16[768,256]{1,0:T(8,128)(2,1)S(1)}, bf16[1280,768]{1,0:T(8,128)(2,1)}) custom-call(s32[4]{0:T(128)S(1)} %pad_add_fusion.meta_ref.refs_6_, bf16[256,768]{1,0:T(8,128)(2,1)S(1)} %get-tuple-element.51.refs_1_.refs_0_, bf16[256,768]{1,0:T(8,128)(2,1)S(1)} %collective-permute-done.14.refs_1_, ...), custom_call_target="tpu_custom_call", output_to_operand_aliasing={{1}: (6, {})} | custom-call | flops 49999998976 | bytes 1000 | tf_op jit(solution)/shard_map/pallas_call | solution.py:325
  85.2 1.6 %collective-permute-start.17 = (bf16[768,256]{1,0:T(8,128)(2,1)S(1)}, bf16[768,256]{1,0:T(8,128)(2,1)S(1)}, u32[]{:S(2)}, u32[]{:S(2)}) collective-permute-start(bf16[768,256]{1,0:T(8,128)(2,1)S(1)} %get-tuple-element.65.refs_4_), channel_id=1, source_target_pairs={{0,4},{4,8},{8,12},{12,0},{1,5},{5,9},{9,13},{13,1},{2,6},{6,10},{... | collective-permute-start | bytes 1179656 | tf_op jit(solution)/shard_map/ppermute | solution.py:405
  86.8 1.8 %collective-permute-done.11.refs_1_ = bf16[256,512]{1,0:T(8,128)(2,1)S(1)} collective-permute-done((bf16[256,512]{1,0:T(8,128)(2,1)S(1)}, bf16[256,512]{1,0:T(8,128)(2,1)S(1)}, u32[]{:S(2)}, u32[]{:S(2)}) %collective-permute-start.11) | collective-permute-done | bytes 262176 | tf_op jit(solution)/shard_map/ppermute | solution.py:390
  88.7 1.4 %shard_map.87 = (bf16[512,256]{1,0:T(8,128)(2,1)S(1)}, bf16[1280,768]{1,0:T(8,128)(2,1)}) custom-call(s32[4]{0:T(128)S(1)} %pad_add_fusion.meta_ref.refs_6_, bf16[256,512]{1,0:T(8,128)(2,1)S(1)} %get-tuple-element.57.refs_3_.refs_0_, bf16[256,512]{1,0:T(8,128)(2,1)S(1)} %collective-permute-done.11.refs_1_, ...), custom_call_target="tpu_custom_call", output_to_operand_aliasing={{1}: (6, {})} | custom-call | flops 1000 | bytes 1000 | tf_op jit(solution)/shard_map/pallas_call | solution.py:325
  90.1 1.6 %collective-permute-start.16 = (bf16[512,256]{1,0:T(8,128)(2,1)S(1)}, bf16[512,256]{1,0:T(8,128)(2,1)S(1)}, u32[]{:S(2)}, u32[]{:S(2)}) collective-permute-start(bf16[512,256]{1,0:T(8,128)(2,1)S(1)} %get-tuple-element.67.refs_1_), channel_id=1, source_target_pairs={{0,4},{4,8},{8,12},{12,0},{1,5},{5,9},{9,13},{13,1},{2,6},{6,10},{... | collective-permute-start | bytes 786440 | tf_op jit(solution)/shard_map/ppermute | solution.py:405
  91.7 7.4 %collective-permute-done.17.refs_0_ = bf16[768,256]{1,0:T(8,128)(2,1)S(1)} collective-permute-done((bf16[768,256]{1,0:T(8,128)(2,1)S(1)}, bf16[768,256]{1,0:T(8,128)(2,1)S(1)}, u32[]{:S(2)}, u32[]{:S(2)}) %collective-permute-start.17) | collective-permute-done | bytes 393248 | tf_op jit(solution)/shard_map/ppermute | solution.py:405
  99.1 1.3 %shard_map.88.refs_1_ = bf16[1280,768]{1,0:T(8,128)(2,1)} custom-call(s32[4]{0:T(128)S(1)} %pad_add_fusion.meta_ref.refs_6_, bf16[768,256]{1,0:T(8,128)(2,1)S(1)} %collective-permute-done.17.refs_0_, bf16[512,256]{1,0:T(8,128)(2,1)S(1)} %get-tuple-element.67.refs_1_, bf16[1280,768]{1,0:T(8,128)(2,1)} %get-tuple-element.68.refs_2_), custom_call_target="tpu_custom_call", output_to_operand_aliasing={{}: (3, {})} | custom-call | flops 1000 | bytes 1000 | tf_op jit(solution)/shard_map/pallas_call | solution.py:325
  100.4 2.4 %collective-permute-done.16.refs_0_ = bf16[512,256]{1,0:T(8,128)(2,1)S(1)} collective-permute-done((bf16[512,256]{1,0:T(8,128)(2,1)S(1)}, bf16[512,256]{1,0:T(8,128)(2,1)S(1)}, u32[]{:S(2)}, u32[]{:S(2)}) %collective-permute-start.16) | collective-permute-done | bytes 262176 | tf_op jit(solution)/shard_map/ppermute | solution.py:405
  102.9 1.3 %shard_map.89 = bf16[1280,768]{1,0:T(8,128)(2,1)} custom-call(s32[4]{0:T(128)S(1)} %pad_add_fusion.meta_ref.refs_6_, bf16[512,256]{1,0:T(8,128)(2,1)S(1)} %collective-permute-done.16.refs_0_, bf16[1280,768]{1,0:T(8,128)(2,1)} %shard_map.88.refs_1_), custom_call_target="tpu_custom_call", output_to_operand_aliasing={{}: (2, {})} | custom-call | flops 1000 | bytes 1000 | tf_op jit(solution)/shard_map/pallas_call | solution.py:325
  (27 shorter events, 5.9 us)
Async XLA Ops:
  1.4 0.7 copy-start
  2.1 10.3 %copy-start.1 = (f32[12,40]{1,0:T(8,128)S(1)}, f32[12,40]{1,0:T(8,128)}, u32[]{:S(2)}) copy-start(f32[12,40]{1,0:T(8,128)} %s_hbm.11) | copy-start | bytes 5764
  10.3 2.2 %collective-permute-start = (bf16[256,1024]{1,0:T(8,128)(2,1)S(1)}, bf16[256,1024]{1,0:T(8,128)(2,1)S(1)}, u32[]{:S(2)}, u32[]{:S(2)}) collective-permute-start(bf16[256,1024]{1,0:T(8,128)(2,1)S(1)} %get-tuple-element.38), channel_id=1, source_target_pairs={{0,1},{1,0},{2,3},{3,2},{4,5},{5,4},{6,7},{7,6},{8,9},{9,8},{10,11... | collective-permute-start | bytes 1572872 | tf_op jit(solution)/shard_map/ppermute | solution.py:382
  10.9 7.7 %collective-permute-start.2 = (bf16[256,1536]{1,0:T(8,128)(2,1)S(1)}, bf16[256,1536]{1,0:T(8,128)(2,1)S(1)}, u32[]{:S(2)}, u32[]{:S(2)}) collective-permute-start(bf16[256,1536]{1,0:T(8,128)(2,1)S(1)} %get-tuple-element.39.refs_1_), channel_id=1, source_target_pairs={{0,1},{1,0},{2,3},{3,2},{4,5},{5,4},{6,7},{7,6},{8,9},{9,8},{10,11... | collective-permute-start | bytes 2359304 | tf_op jit(solution)/shard_map/ppermute | solution.py:382
  15.7 9.5 %collective-permute-start.1 = (bf16[256,512]{1,0:T(8,128)(2,1)S(1)}, bf16[256,512]{1,0:T(8,128)(2,1)S(1)}, u32[]{:S(2)}, u32[]{:S(2)}) collective-permute-start(bf16[256,512]{1,0:T(8,128)(2,1)S(1)} %get-tuple-element.41), channel_id=1, source_target_pairs={{0,2},{1,3},{2,0},{3,1},{4,6},{5,7},{6,4},{7,5},{8,10},{9,11},{10,... | collective-permute-start | bytes 786440 | tf_op jit(solution)/shard_map/ppermute | solution.py:390
  23.0 23.0 %collective-permute-start.6 = (bf16[256,768]{1,0:T(8,128)(2,1)S(1)}, bf16[256,768]{1,0:T(8,128)(2,1)S(1)}, u32[]{:S(2)}, u32[]{:S(2)}) collective-permute-start(bf16[256,768]{1,0:T(8,128)(2,1)S(1)} %get-tuple-element.49), channel_id=1, source_target_pairs={{0,2},{1,3},{2,0},{3,1},{4,6},{5,7},{6,4},{7,5},{8,10},{9,11},{10,... | collective-permute-start | bytes 1179656 | tf_op jit(solution)/shard_map/ppermute | solution.py:390
  26.0 20.0 %collective-permute-start.7 = (bf16[512,256]{1,0:T(8,128)(2,1)S(1)}, bf16[512,256]{1,0:T(8,128)(2,1)S(1)}, u32[]{:S(2)}, u32[]{:S(2)}) collective-permute-start(bf16[512,256]{1,0:T(8,128)(2,1)S(1)} %shard_map.76.refs_6_.refs_2_), channel_id=1, source_target_pairs={{0,8},{4,12},{8,0},{12,4},{1,9},{5,13},{9,1},{13,5},{2,10},{6,14},... | collective-permute-start | bytes 786440 | tf_op jit(solution)/shard_map/ppermute | solution.py:405
  37.1 21.6 %collective-permute-start.10 = (bf16[256,1536]{1,0:T(8,128)(2,1)S(1)}, bf16[256,1536]{1,0:T(8,128)(2,1)S(1)}, u32[]{:S(2)}, u32[]{:S(2)}) collective-permute-start(bf16[256,1536]{1,0:T(8,128)(2,1)S(1)} %get-tuple-element.43.refs_6_), channel_id=1, source_target_pairs={{0,1},{1,0},{2,3},{3,2},{4,5},{5,4},{6,7},{7,6},{8,9},{9,8},{10,11... | collective-permute-start | bytes 2359304 | tf_op jit(solution)/shard_map/ppermute | solution.py:382
  45.4 7.6 %collective-permute-start.4 = (bf16[256,1024]{1,0:T(8,128)(2,1)S(1)}, bf16[256,1024]{1,0:T(8,128)(2,1)S(1)}, u32[]{:S(2)}, u32[]{:S(2)}) collective-permute-start(bf16[256,1024]{1,0:T(8,128)(2,1)S(1)} %get-tuple-element.47), channel_id=1, source_target_pairs={{0,1},{1,0},{2,3},{3,2},{4,5},{5,4},{6,7},{7,6},{8,9},{9,8},{10,11... | collective-permute-start | bytes 1572872 | tf_op jit(solution)/shard_map/ppermute | solution.py:382
  45.9 2.7 %collective-permute-start.5 = (bf16[256,1536]{1,0:T(8,128)(2,1)S(1)}, bf16[256,1536]{1,0:T(8,128)(2,1)S(1)}, u32[]{:S(2)}, u32[]{:S(2)}) collective-permute-start(bf16[256,1536]{1,0:T(8,128)(2,1)S(1)} %get-tuple-element.48.refs_3_), channel_id=1, source_target_pairs={{0,1},{1,0},{2,3},{3,2},{4,5},{5,4},{6,7},{7,6},{8,9},{9,8},{10,11... | collective-permute-start | bytes 2359304 | tf_op jit(solution)/shard_map/ppermute | solution.py:382
  46.9 20.9 %collective-permute-start.9 = (bf16[768,256]{1,0:T(8,128)(2,1)S(1)}, bf16[768,256]{1,0:T(8,128)(2,1)S(1)}, u32[]{:S(2)}, u32[]{:S(2)}) collective-permute-start(bf16[768,256]{1,0:T(8,128)(2,1)S(1)} %get-tuple-element.50.refs_1_.refs_2_), channel_id=1, source_target_pairs={{0,8},{4,12},{8,0},{12,4},{1,9},{5,13},{9,1},{13,5},{2,10},{6,14},... | collective-permute-start | bytes 1179656 | tf_op jit(solution)/shard_map/ppermute | solution.py:405
  56.2 11.5 %collective-permute-start.8 = (bf16[256,512]{1,0:T(8,128)(2,1)S(1)}, bf16[256,512]{1,0:T(8,128)(2,1)S(1)}, u32[]{:S(2)}, u32[]{:S(2)}) collective-permute-start(bf16[256,512]{1,0:T(8,128)(2,1)S(1)} %get-tuple-element.53), channel_id=1, source_target_pairs={{0,2},{1,3},{2,0},{3,1},{4,6},{5,7},{6,4},{7,5},{8,10},{9,11},{10,... | collective-permute-start | bytes 786440 | tf_op jit(solution)/shard_map/ppermute | solution.py:390
  58.7 11.1 %collective-permute-start.3 = (bf16[256,1024]{1,0:T(8,128)(2,1)S(1)}, bf16[256,1024]{1,0:T(8,128)(2,1)S(1)}, u32[]{:S(2)}, u32[]{:S(2)}) collective-permute-start(bf16[256,1024]{1,0:T(8,128)(2,1)S(1)} %get-tuple-element.45), channel_id=1, source_target_pairs={{0,1},{1,0},{2,3},{3,2},{4,5},{5,4},{6,7},{7,6},{8,9},{9,8},{10,11... | collective-permute-start | bytes 1572872 | tf_op jit(solution)/shard_map/ppermute | solution.py:382
  63.1 12.5 %collective-permute-start.12 = (bf16[256,768]{1,0:T(8,128)(2,1)S(1)}, bf16[256,768]{1,0:T(8,128)(2,1)S(1)}, u32[]{:S(2)}, u32[]{:S(2)}) collective-permute-start(bf16[256,768]{1,0:T(8,128)(2,1)S(1)} %get-tuple-element.60), channel_id=1, source_target_pairs={{0,2},{1,3},{2,0},{3,1},{4,6},{5,7},{6,4},{7,5},{8,10},{9,11},{10,... | collective-permute-start | bytes 1179656 | tf_op jit(solution)/shard_map/ppermute | solution.py:390
  63.5 20.0 %collective-permute-start.14 = (bf16[256,768]{1,0:T(8,128)(2,1)S(1)}, bf16[256,768]{1,0:T(8,128)(2,1)S(1)}, u32[]{:S(2)}, u32[]{:S(2)}) collective-permute-start(bf16[256,768]{1,0:T(8,128)(2,1)S(1)} %get-tuple-element.62), channel_id=1, source_target_pairs={{0,2},{1,3},{2,0},{3,1},{4,6},{5,7},{6,4},{7,5},{8,10},{9,11},{10,... | collective-permute-start | bytes 1179656 | tf_op jit(solution)/shard_map/ppermute | solution.py:390
  68.5 15.0 %collective-permute-start.15 = (bf16[512,256]{1,0:T(8,128)(2,1)S(1)}, bf16[512,256]{1,0:T(8,128)(2,1)S(1)}, u32[]{:S(2)}, u32[]{:S(2)}) collective-permute-start(bf16[512,256]{1,0:T(8,128)(2,1)S(1)} %get-tuple-element.56.refs_1_), channel_id=1, source_target_pairs={{0,12},{4,0},{8,4},{12,8},{1,13},{5,1},{9,5},{13,9},{2,14},{6,2},{... | collective-permute-start | bytes 786440 | tf_op jit(solution)/shard_map/ppermute | solution.py:405
  73.1 15.6 %collective-permute-start.11 = (bf16[256,512]{1,0:T(8,128)(2,1)S(1)}, bf16[256,512]{1,0:T(8,128)(2,1)S(1)}, u32[]{:S(2)}, u32[]{:S(2)}) collective-permute-start(bf16[256,512]{1,0:T(8,128)(2,1)S(1)} %get-tuple-element.58), channel_id=1, source_target_pairs={{0,2},{1,3},{2,0},{3,1},{4,6},{5,7},{6,4},{7,5},{8,10},{9,11},{10,... | collective-permute-start | bytes 786440 | tf_op jit(solution)/shard_map/ppermute | solution.py:390
  76.7 12.0 %collective-permute-start.13 = (bf16[768,256]{1,0:T(8,128)(2,1)S(1)}, bf16[768,256]{1,0:T(8,128)(2,1)S(1)}, u32[]{:S(2)}, u32[]{:S(2)}) collective-permute-start(bf16[768,256]{1,0:T(8,128)(2,1)S(1)} %get-tuple-element.61.refs_4_), channel_id=1, source_target_pairs={{0,12},{4,0},{8,4},{12,8},{1,13},{5,1},{9,5},{13,9},{2,14},{6,2},{... | collective-permute-start | bytes 1179656 | tf_op jit(solution)/shard_map/ppermute | solution.py:405
  85.2 13.9 %collective-permute-start.17 = (bf16[768,256]{1,0:T(8,128)(2,1)S(1)}, bf16[768,256]{1,0:T(8,128)(2,1)S(1)}, u32[]{:S(2)}, u32[]{:S(2)}) collective-permute-start(bf16[768,256]{1,0:T(8,128)(2,1)S(1)} %get-tuple-element.65.refs_4_), channel_id=1, source_target_pairs={{0,4},{4,8},{8,12},{12,0},{1,5},{5,9},{9,13},{13,1},{2,6},{6,10},{... | collective-permute-start | bytes 1179656 | tf_op jit(solution)/shard_map/ppermute | solution.py:405
  90.1 12.8 %collective-permute-start.16 = (bf16[512,256]{1,0:T(8,128)(2,1)S(1)}, bf16[512,256]{1,0:T(8,128)(2,1)S(1)}, u32[]{:S(2)}, u32[]{:S(2)}) collective-permute-start(bf16[512,256]{1,0:T(8,128)(2,1)S(1)} %get-tuple-element.67.refs_1_), channel_id=1, source_target_pairs={{0,4},{4,8},{8,12},{12,0},{1,5},{5,9},{9,13},{13,1},{2,6},{6,10},{... | collective-permute-start | bytes 786440 | tf_op jit(solution)/shard_map/ppermute | solution.py:405

commit v2 on v1

--- a/solution.py
+++ b/solution.py
@@ -16,6 +16,7 @@
 HEADS_STEP = 4
 
 ANY = pl.BlockSpec(memory_space=pl.ANY)
+HBM = pl.BlockSpec(memory_space=pltpu.HBM)
 
 
 def params():
@@ -175,7 +176,7 @@
         grid_spec=pltpu.PrefetchScalarGridSpec(
             num_scalar_prefetch=1,
             grid=(1,),
-            in_specs=[ANY] * len(operands),
+            in_specs=([HBM] * 4 if attend else [ANY]) + [HBM, HBM, ANY],
             out_specs=[ANY] * len(shapes),
             scratch_shapes=scratch + [pltpu.SemaphoreType.DMA],
         ),
@@ -240,7 +241,7 @@
         grid_spec=pltpu.PrefetchScalarGridSpec(
             num_scalar_prefetch=1,
             grid=(1,),
-            in_specs=[ANY] * (4 + len(received)),
+            in_specs=[ANY, HBM, HBM] + [ANY] * (1 + len(received)),
             out_specs=[ANY] * 2,
             scratch_shapes=[
                 pltpu.VMEM((rows, depth), bf16),

time: 105 us -> 104 us (level)
  transfers between devices with their start and end apart: 18 -> 18, of which waited for: 8 -> 8; matrix products, arithmetic and copies ran while one was open for 0% -> 0% of each run, Pallas kernels for 45% -> 46%
where the time goes in v2:
time: 104 us
  Pallas kernels  57.7 us (55%)
  waiting for transfers between devices  24.1 us (23%)
  starting transfers between devices  20.2 us (19%)
  local copies, waits for them, and re-layouts  1.39 us (1%)
    pallas_call x3, Pallas kernels, sibling_part(): pl.pallas_call(functools.partial(sibling_kernel, features, slot, ranges,...  24.6 us
    pallas_call x6, Pallas kernels, own_part(): pl.pallas_call(functools.partial(own_kernel, features, chunk, len(receive...  22.9 us
    ppermute x6, waiting for transfers between devices, pipeline(): lax.ppermute(token, 'dp', [(i, (i + SHIFTS[slot]) % groups) for i in rang...  12.9 us
    pallas_call x8, Pallas kernels, finish(): pl.pallas_call(functools.partial(finish_kernel, slot, first, into, [a[:2]...  10.1 us
    ppermute x6, starting transfers between devices, pipeline(): from_chip[index] = lax.ppermute(send, 'tensor', other_chip)  9.9 us
    ppermute x6, starting transfers between devices, pipeline(): lax.ppermute(token, 'dp', [(i, (i + SHIFTS[slot]) % groups) for i in rang...  8.78 us
    ppermute x6, waiting for transfers between devices, pipeline(): from_chip[index] = lax.ppermute(send, 'tensor', other_chip)  8.75 us
    ppermute x6, waiting for transfers between devices, pipeline(): lax.ppermute(array, 'tensor', other_core)  2.46 us
  transfers between devices with their start and end apart: 18, of which 8 were waited for; matrix products, arithmetic and copies ran while one was open for 0% of the time, Pallas kernels for 46%

profile of v2, /device:TPU:0, one launch (start us, length us, event | category | flops | bytes accessed | tf_op | source)
XLA Modules:
  0.0 104.3 jit_solution(10958130220937641904)
XLA Ops:
  2.1 8.1 %shard_map.73 = (bf16[256,1536]{1,0:T(8,128)(2,1)S(1)}, bf16[256,1024]{1,0:T(8,128)(2,1)S(1)}, bf16[256,1536]{1,0:T(8,128)(2,1)S(1)}) custom-call(s32[4]{0:T(128)S(1)} %pad_add_fusion.meta_ref.refs_6_, bf16[768,1536]{1,0:T(8,128)(2,1)} %refs_0_.5, bf16[768,1536]{1,0:T(8,128)(2,1)} %refs_1_.5, bf16[768,1536]{1,0:T(8,128)(2,1)} %refs_2_.5, ...), custom_call_target="tpu_custom_call" | custom-call | flops 49999998976 | bytes 1000 | tf_op jit(solution)/shard_map/pallas_call | solution.py:174
  10.9 1.5 %collective-permute-done.refs_0_ = bf16[256,1024]{1,0:T(8,128)(2,1)S(1)} collective-permute-done((bf16[256,1024]{1,0:T(8,128)(2,1)S(1)}, bf16[256,1024]{1,0:T(8,128)(2,1)S(1)}, u32[]{:S(2)}, u32[]{:S(2)}) %collective-permute-start) | collective-permute-done | bytes 524320 | tf_op jit(solution)/shard_map/ppermute | solution.py:383
  12.3 3.3 %shard_map.74 = (bf16[256,512]{1,0:T(8,128)(2,1)S(1)}, bf16[256,512]{1,0:T(8,128)(2,1)S(1)}) custom-call(s32[4]{0:T(128)S(1)} %pad_add_fusion.meta_ref.refs_6_, bf16[256,1536]{1,0:T(8,128)(2,1)S(1)} %get-tuple-element.37.att_hbm, bf16[1536,5120]{1,0:T(8,128)(2,1)} %w_hbm.11, f32[12,40]{1,0:T(8,128)S(1)} %copy-done.1, ...), custom_call_target="tpu_custom_call" | custom-call | flops 49999998976 | bytes 1000 | tf_op jit(solution)/shard_map/pallas_call | solution.py:239
  15.6 3.0 %collective-permute-start.1 = (bf16[256,512]{1,0:T(8,128)(2,1)S(1)}, bf16[256,512]{1,0:T(8,128)(2,1)S(1)}, u32[]{:S(2)}, u32[]{:S(2)}) collective-permute-start(bf16[256,512]{1,0:T(8,128)(2,1)S(1)} %get-tuple-element.41), channel_id=1, source_target_pairs={{0,2},{1,3},{2,0},{3,1},{4,6},{5,7},{6,4},{7,5},{8,10},{9,11},{10,... | collective-permute-start | bytes 786440 | tf_op jit(solution)/shard_map/ppermute | solution.py:391
  18.6 4.3 %shard_map.75 = (bf16[256,768]{1,0:T(8,128)(2,1)S(1)}, bf16[256,768]{1,0:T(8,128)(2,1)S(1)}) custom-call(s32[4]{0:T(128)S(1)} %pad_add_fusion.meta_ref.refs_6_, bf16[256,1536]{1,0:T(8,128)(2,1)S(1)} %get-tuple-element.37.att_hbm, bf16[1536,5120]{1,0:T(8,128)(2,1)} %w_hbm.11, f32[12,40]{1,0:T(8,128)S(1)} %copy-done.1, ...), custom_call_target="tpu_custom_call" | custom-call | flops 49999998976 | bytes 1000 | tf_op jit(solution)/shard_map/pallas_call | solution.py:239
  23.1 2.2 %collective-permute-done.1.refs_1_ = bf16[256,512]{1,0:T(8,128)(2,1)S(1)} collective-permute-done((bf16[256,512]{1,0:T(8,128)(2,1)S(1)}, bf16[256,512]{1,0:T(8,128)(2,1)S(1)}, u32[]{:S(2)}, u32[]{:S(2)}) %collective-permute-start.1) | collective-permute-done | bytes 262176 | tf_op jit(solution)/shard_map/ppermute | solution.py:391
  26.0 2.8 %collective-permute-start.7 = (bf16[512,256]{1,0:T(8,128)(2,1)S(1)}, bf16[512,256]{1,0:T(8,128)(2,1)S(1)}, u32[]{:S(2)}, u32[]{:S(2)}) collective-permute-start(bf16[512,256]{1,0:T(8,128)(2,1)S(1)} %shard_map.76.refs_6_.refs_2_), channel_id=1, source_target_pairs={{0,8},{4,12},{8,0},{12,4},{1,9},{5,13},{9,1},{13,5},{2,10},{6,14},... | collective-permute-start | bytes 786440 | tf_op jit(solution)/shard_map/ppermute | solution.py:406
  28.8 8.3 %shard_map.77 = (bf16[256,1536]{1,0:T(8,128)(2,1)S(1)}, bf16[256,1024]{1,0:T(8,128)(2,1)S(1)}, bf16[256,1536]{1,0:T(8,128)(2,1)S(1)}) custom-call(s32[4]{0:T(128)S(1)} %pad_add_fusion.meta_ref.refs_6_, bf16[768,1536]{1,0:T(8,128)(2,1)} %refs_0_.5, bf16[768,1536]{1,0:T(8,128)(2,1)} %refs_1_.5, bf16[768,1536]{1,0:T(8,128)(2,1)} %refs_2_.5, ...), custom_call_target="tpu_custom_call" | custom-call | flops 1000 | bytes 1000 | tf_op jit(solution)/shard_map/pallas_call | solution.py:174
  37.2 8.1 %shard_map.78 = (bf16[256,1536]{1,0:T(8,128)(2,1)S(1)}, bf16[256,1024]{1,0:T(8,128)(2,1)S(1)}, bf16[256,1536]{1,0:T(8,128)(2,1)S(1)}) custom-call(s32[4]{0:T(128)S(1)} %pad_add_fusion.meta_ref.refs_6_, bf16[768,1536]{1,0:T(8,128)(2,1)} %refs_0_.5, bf16[768,1536]{1,0:T(8,128)(2,1)} %refs_1_.5, bf16[768,1536]{1,0:T(8,128)(2,1)} %refs_2_.5, ...), custom_call_target="tpu_custom_call" | custom-call | flops 1000 | bytes 1000 | tf_op jit(solution)/shard_map/pallas_call | solution.py:174
  46.1 1.3 %shard_map.79 = (bf16[768,256]{1,0:T(8,128)(2,1)S(1)}, bf16[1280,768]{1,0:T(8,128)(2,1)}) custom-call(s32[4]{0:T(128)S(1)} %pad_add_fusion.meta_ref.refs_6_, bf16[256,768]{1,0:T(8,128)(2,1)S(1)} %get-tuple-element.42.refs_2_.refs_0_, bf16[256,768]{1,0:T(8,128)(2,1)S(1)} %collective-permute-done.6.refs_1_, ...), custom_call_target="tpu_custom_call" | custom-call | flops 49999998976 | bytes 1000 | tf_op jit(solution)/shard_map/pallas_call | solution.py:326
  48.7 4.3 %shard_map.80 = (bf16[256,768]{1,0:T(8,128)(2,1)S(1)}, bf16[256,768]{1,0:T(8,128)(2,1)S(1)}) custom-call(s32[4]{0:T(128)S(1)} %pad_add_fusion.meta_ref.refs_6_, bf16[256,1536]{1,0:T(8,128)(2,1)S(1)} %get-tuple-element.44.att_hbm, bf16[1536,5120]{1,0:T(8,128)(2,1)} %w_hbm.11, f32[12,40]{1,0:T(8,128)S(1)} %copy-done.1, ...), custom_call_target="tpu_custom_call" | custom-call | flops 49999998976 | bytes 1000 | tf_op jit(solution)/shard_map/pallas_call | solution.py:239
  53.0 3.3 %shard_map.81 = (bf16[256,512]{1,0:T(8,128)(2,1)S(1)}, bf16[256,512]{1,0:T(8,128)(2,1)S(1)}) custom-call(s32[4]{0:T(128)S(1)} %pad_add_fusion.meta_ref.refs_6_, bf16[256,1536]{1,0:T(8,128)(2,1)S(1)} %get-tuple-element.46.att_hbm, bf16[1536,5120]{1,0:T(8,128)(2,1)} %w_hbm.11, f32[12,40]{1,0:T(8,128)S(1)} %copy-done.1, ...), custom_call_target="tpu_custom_call" | custom-call | flops 1000 | bytes 1000 | tf_op jit(solution)/shard_map/pallas_call | solution.py:239
  56.3 2.3 %collective-permute-start.8 = (bf16[256,512]{1,0:T(8,128)(2,1)S(1)}, bf16[256,512]{1,0:T(8,128)(2,1)S(1)}, u32[]{:S(2)}, u32[]{:S(2)}) collective-permute-start(bf16[256,512]{1,0:T(8,128)(2,1)S(1)} %get-tuple-element.53), channel_id=1, source_target_pairs={{0,2},{1,3},{2,0},{3,1},{4,6},{5,7},{6,4},{7,5},{8,10},{9,11},{10,... | collective-permute-start | bytes 786440 | tf_op jit(solution)/shard_map/ppermute | solution.py:391
  58.8 4.3 %shard_map.82 = (bf16[256,768]{1,0:T(8,128)(2,1)S(1)}, bf16[256,768]{1,0:T(8,128)(2,1)S(1)}) custom-call(s32[4]{0:T(128)S(1)} %pad_add_fusion.meta_ref.refs_6_, bf16[256,1536]{1,0:T(8,128)(2,1)S(1)} %get-tuple-element.46.att_hbm, bf16[1536,5120]{1,0:T(8,128)(2,1)} %w_hbm.11, f32[12,40]{1,0:T(8,128)S(1)} %copy-done.1, ...), custom_call_target="tpu_custom_call" | custom-call | flops 1000 | bytes 1000 | tf_op jit(solution)/shard_map/pallas_call | solution.py:239
  63.5 1.7 %collective-permute-start.14 = (bf16[256,768]{1,0:T(8,128)(2,1)S(1)}, bf16[256,768]{1,0:T(8,128)(2,1)S(1)}, u32[]{:S(2)}, u32[]{:S(2)}) collective-permute-start(bf16[256,768]{1,0:T(8,128)(2,1)S(1)} %get-tuple-element.62), channel_id=1, source_target_pairs={{0,2},{1,3},{2,0},{3,1},{4,6},{5,7},{6,4},{7,5},{8,10},{9,11},{10,... | collective-permute-start | bytes 1179656 | tf_op jit(solution)/shard_map/ppermute | solution.py:391
  65.2 3.0 %collective-permute-done.9.refs_3_ = bf16[768,256]{1,0:T(8,128)(2,1)S(1)} collective-permute-done((bf16[768,256]{1,0:T(8,128)(2,1)S(1)}, bf16[768,256]{1,0:T(8,128)(2,1)S(1)}, u32[]{:S(2)}, u32[]{:S(2)}) %collective-permute-start.9) | collective-permute-done | bytes 393248 | tf_op jit(solution)/shard_map/ppermute | solution.py:406
  68.3 1.3 %shard_map.83 = (bf16[512,256]{1,0:T(8,128)(2,1)S(1)}, bf16[512,256]{1,0:T(8,128)(2,1)S(1)}, bf16[1280,768]{1,0:T(8,128)(2,1)}) custom-call(s32[4]{0:T(128)S(1)} %pad_add_fusion.meta_ref.refs_6_, bf16[256,512]{1,0:T(8,128)(2,1)S(1)} %get-tuple-element.52.refs_1_.refs_0_, ...), custom_call_target="tpu_custom_call", output_to_operand_aliasing={{2}: (6, {})} | custom-call | flops 49999998976 | bytes 1000 | tf_op jit(solution)/shard_map/pallas_call | solution.py:326
  69.6 1.2 %collective-permute-start.15 = (bf16[512,256]{1,0:T(8,128)(2,1)S(1)}, bf16[512,256]{1,0:T(8,128)(2,1)S(1)}, u32[]{:S(2)}, u32[]{:S(2)}) collective-permute-start(bf16[512,256]{1,0:T(8,128)(2,1)S(1)} %get-tuple-element.56.refs_1_), channel_id=1, source_target_pairs={{0,12},{4,0},{8,4},{12,8},{1,13},{5,1},{9,5},{13,9},{2,14},{6,2},{... | collective-permute-start | bytes 786440 | tf_op jit(solution)/shard_map/ppermute | solution.py:406
  70.8 3.3 %shard_map.84 = (bf16[256,512]{1,0:T(8,128)(2,1)S(1)}, bf16[256,512]{1,0:T(8,128)(2,1)S(1)}) custom-call(s32[4]{0:T(128)S(1)} %pad_add_fusion.meta_ref.refs_6_, bf16[256,1536]{1,0:T(8,128)(2,1)S(1)} %get-tuple-element.44.att_hbm, bf16[1536,5120]{1,0:T(8,128)(2,1)} %w_hbm.11, f32[12,40]{1,0:T(8,128)S(1)} %copy-done.1, ...), custom_call_target="tpu_custom_call" | custom-call | flops 1000 | bytes 1000 | tf_op jit(solution)/shard_map/pallas_call | solution.py:239
  74.1 2.4 %collective-permute-start.11 = (bf16[256,512]{1,0:T(8,128)(2,1)S(1)}, bf16[256,512]{1,0:T(8,128)(2,1)S(1)}, u32[]{:S(2)}, u32[]{:S(2)}) collective-permute-start(bf16[256,512]{1,0:T(8,128)(2,1)S(1)} %get-tuple-element.58), channel_id=1, source_target_pairs={{0,2},{1,3},{2,0},{3,1},{4,6},{5,7},{6,4},{7,5},{8,10},{9,11},{10,... | collective-permute-start | bytes 786440 | tf_op jit(solution)/shard_map/ppermute | solution.py:391
  76.5 1.1 %shard_map.85 = (bf16[768,256]{1,0:T(8,128)(2,1)S(1)}, bf16[768,256]{1,0:T(8,128)(2,1)S(1)}) custom-call(s32[4]{0:T(128)S(1)} %pad_add_fusion.meta_ref.refs_6_, bf16[256,768]{1,0:T(8,128)(2,1)S(1)} %get-tuple-element.54.refs_4_.refs_0_, bf16[256,768]{1,0:T(8,128)(2,1)S(1)} %collective-permute-done.12.refs_1_, ...), custom_call_target="tpu_custom_call" | custom-call | flops 1000 | bytes 1000 | tf_op jit(solution)/shard_map/pallas_call | solution.py:326
  77.6 1.3 %collective-permute-start.13 = (bf16[768,256]{1,0:T(8,128)(2,1)S(1)}, bf16[768,256]{1,0:T(8,128)(2,1)S(1)}, u32[]{:S(2)}, u32[]{:S(2)}) collective-permute-start(bf16[768,256]{1,0:T(8,128)(2,1)S(1)} %get-tuple-element.61.refs_4_), channel_id=1, source_target_pairs={{0,12},{4,0},{8,4},{12,8},{1,13},{5,1},{9,5},{13,9},{2,14},{6,2},{... | collective-permute-start | bytes 1179656 | tf_op jit(solution)/shard_map/ppermute | solution.py:406
  78.9 4.7 %collective-permute-done.14.refs_1_ = bf16[256,768]{1,0:T(8,128)(2,1)S(1)} collective-permute-done((bf16[256,768]{1,0:T(8,128)(2,1)S(1)}, bf16[256,768]{1,0:T(8,128)(2,1)S(1)}, u32[]{:S(2)}, u32[]{:S(2)}) %collective-permute-start.14) | collective-permute-done | bytes 393248 | tf_op jit(solution)/shard_map/ppermute | solution.py:391
  83.5 1.7 %shard_map.86 = (bf16[768,256]{1,0:T(8,128)(2,1)S(1)}, bf16[1280,768]{1,0:T(8,128)(2,1)}) custom-call(s32[4]{0:T(128)S(1)} %pad_add_fusion.meta_ref.refs_6_, bf16[256,768]{1,0:T(8,128)(2,1)S(1)} %get-tuple-element.51.refs_1_.refs_0_, bf16[256,768]{1,0:T(8,128)(2,1)S(1)} %collective-permute-done.14.refs_1_, ...), custom_call_target="tpu_custom_call", output_to_operand_aliasing={{1}: (6, {})} | custom-call | flops 49999998976 | bytes 1000 | tf_op jit(solution)/shard_map/pallas_call | solution.py:326
  85.2 1.6 %collective-permute-start.17 = (bf16[768,256]{1,0:T(8,128)(2,1)S(1)}, bf16[768,256]{1,0:T(8,128)(2,1)S(1)}, u32[]{:S(2)}, u32[]{:S(2)}) collective-permute-start(bf16[768,256]{1,0:T(8,128)(2,1)S(1)} %get-tuple-element.65.refs_4_), channel_id=1, source_target_pairs={{0,4},{4,8},{8,12},{12,0},{1,5},{5,9},{9,13},{13,1},{2,6},{6,10},{... | collective-permute-start | bytes 1179656 | tf_op jit(solution)/shard_map/ppermute | solution.py:406
  86.8 1.9 %collective-permute-done.11.refs_1_ = bf16[256,512]{1,0:T(8,128)(2,1)S(1)} collective-permute-done((bf16[256,512]{1,0:T(8,128)(2,1)S(1)}, bf16[256,512]{1,0:T(8,128)(2,1)S(1)}, u32[]{:S(2)}, u32[]{:S(2)}) %collective-permute-start.11) | collective-permute-done | bytes 262176 | tf_op jit(solution)/shard_map/ppermute | solution.py:391
  88.7 1.4 %shard_map.87 = (bf16[512,256]{1,0:T(8,128)(2,1)S(1)}, bf16[1280,768]{1,0:T(8,128)(2,1)}) custom-call(s32[4]{0:T(128)S(1)} %pad_add_fusion.meta_ref.refs_6_, bf16[256,512]{1,0:T(8,128)(2,1)S(1)} %get-tuple-element.57.refs_3_.refs_0_, bf16[256,512]{1,0:T(8,128)(2,1)S(1)} %collective-permute-done.11.refs_1_, ...), custom_call_target="tpu_custom_call", output_to_operand_aliasing={{1}: (6, {})} | custom-call | flops 1000 | bytes 1000 | tf_op jit(solution)/shard_map/pallas_call | solution.py:326
  90.1 1.6 %collective-permute-start.16 = (bf16[512,256]{1,0:T(8,128)(2,1)S(1)}, bf16[512,256]{1,0:T(8,128)(2,1)S(1)}, u32[]{:S(2)}, u32[]{:S(2)}) collective-permute-start(bf16[512,256]{1,0:T(8,128)(2,1)S(1)} %get-tuple-element.67.refs_1_), channel_id=1, source_target_pairs={{0,4},{4,8},{8,12},{12,0},{1,5},{5,9},{9,13},{13,1},{2,6},{6,10},{... | collective-permute-start | bytes 786440 | tf_op jit(solution)/shard_map/ppermute | solution.py:406
  91.7 7.4 %collective-permute-done.17.refs_0_ = bf16[768,256]{1,0:T(8,128)(2,1)S(1)} collective-permute-done((bf16[768,256]{1,0:T(8,128)(2,1)S(1)}, bf16[768,256]{1,0:T(8,128)(2,1)S(1)}, u32[]{:S(2)}, u32[]{:S(2)}) %collective-permute-start.17) | collective-permute-done | bytes 393248 | tf_op jit(solution)/shard_map/ppermute | solution.py:406
  99.1 1.3 %shard_map.88.refs_1_ = bf16[1280,768]{1,0:T(8,128)(2,1)} custom-call(s32[4]{0:T(128)S(1)} %pad_add_fusion.meta_ref.refs_6_, bf16[768,256]{1,0:T(8,128)(2,1)S(1)} %collective-permute-done.17.refs_0_, bf16[512,256]{1,0:T(8,128)(2,1)S(1)} %get-tuple-element.67.refs_1_, bf16[1280,768]{1,0:T(8,128)(2,1)} %get-tuple-element.68.refs_2_), custom_call_target="tpu_custom_call", output_to_operand_aliasing={{}: (3, {})} | custom-call | flops 1000 | bytes 1000 | tf_op jit(solution)/shard_map/pallas_call | solution.py:326
  100.5 2.4 %collective-permute-done.16.refs_0_ = bf16[512,256]{1,0:T(8,128)(2,1)S(1)} collective-permute-done((bf16[512,256]{1,0:T(8,128)(2,1)S(1)}, bf16[512,256]{1,0:T(8,128)(2,1)S(1)}, u32[]{:S(2)}, u32[]{:S(2)}) %collective-permute-start.16) | collective-permute-done | bytes 262176 | tf_op jit(solution)/shard_map/ppermute | solution.py:406
  102.9 1.3 %shard_map.89 = bf16[1280,768]{1,0:T(8,128)(2,1)} custom-call(s32[4]{0:T(128)S(1)} %pad_add_fusion.meta_ref.refs_6_, bf16[512,256]{1,0:T(8,128)(2,1)S(1)} %collective-permute-done.16.refs_0_, bf16[1280,768]{1,0:T(8,128)(2,1)} %shard_map.88.refs_1_), custom_call_target="tpu_custom_call", output_to_operand_aliasing={{}: (2, {})} | custom-call | flops 1000 | bytes 1000 | tf_op jit(solution)/shard_map/pallas_call | solution.py:326
  (27 shorter events, 6.2 us)
Async XLA Ops:
  1.4 0.7 copy-start
  2.1 10.2 %copy-start.1 = (f32[12,40]{1,0:T(8,128)S(1)}, f32[12,40]{1,0:T(8,128)}, u32[]{:S(2)}) copy-start(f32[12,40]{1,0:T(8,128)} %s_hbm.11) | copy-start | bytes 5764
  10.3 2.1 %collective-permute-start = (bf16[256,1024]{1,0:T(8,128)(2,1)S(1)}, bf16[256,1024]{1,0:T(8,128)(2,1)S(1)}, u32[]{:S(2)}, u32[]{:S(2)}) collective-permute-start(bf16[256,1024]{1,0:T(8,128)(2,1)S(1)} %get-tuple-element.38), channel_id=1, source_target_pairs={{0,1},{1,0},{2,3},{3,2},{4,5},{5,4},{6,7},{7,6},{8,9},{9,8},{10,11... | collective-permute-start | bytes 1572872 | tf_op jit(solution)/shard_map/ppermute | solution.py:383
  10.8 7.9 %collective-permute-start.2 = (bf16[256,1536]{1,0:T(8,128)(2,1)S(1)}, bf16[256,1536]{1,0:T(8,128)(2,1)S(1)}, u32[]{:S(2)}, u32[]{:S(2)}) collective-permute-start(bf16[256,1536]{1,0:T(8,128)(2,1)S(1)} %get-tuple-element.39.refs_1_), channel_id=1, source_target_pairs={{0,1},{1,0},{2,3},{3,2},{4,5},{5,4},{6,7},{7,6},{8,9},{9,8},{10,11... | collective-permute-start | bytes 2359304 | tf_op jit(solution)/shard_map/ppermute | solution.py:383
  15.6 9.7 %collective-permute-start.1 = (bf16[256,512]{1,0:T(8,128)(2,1)S(1)}, bf16[256,512]{1,0:T(8,128)(2,1)S(1)}, u32[]{:S(2)}, u32[]{:S(2)}) collective-permute-start(bf16[256,512]{1,0:T(8,128)(2,1)S(1)} %get-tuple-element.41), channel_id=1, source_target_pairs={{0,2},{1,3},{2,0},{3,1},{4,6},{5,7},{6,4},{7,5},{8,10},{9,11},{10,... | collective-permute-start | bytes 786440 | tf_op jit(solution)/shard_map/ppermute | solution.py:391
  23.0 23.1 %collective-permute-start.6 = (bf16[256,768]{1,0:T(8,128)(2,1)S(1)}, bf16[256,768]{1,0:T(8,128)(2,1)S(1)}, u32[]{:S(2)}, u32[]{:S(2)}) collective-permute-start(bf16[256,768]{1,0:T(8,128)(2,1)S(1)} %get-tuple-element.49), channel_id=1, source_target_pairs={{0,2},{1,3},{2,0},{3,1},{4,6},{5,7},{6,4},{7,5},{8,10},{9,11},{10,... | collective-permute-start | bytes 1179656 | tf_op jit(solution)/shard_map/ppermute | solution.py:391
  26.0 20.1 %collective-permute-start.7 = (bf16[512,256]{1,0:T(8,128)(2,1)S(1)}, bf16[512,256]{1,0:T(8,128)(2,1)S(1)}, u32[]{:S(2)}, u32[]{:S(2)}) collective-permute-start(bf16[512,256]{1,0:T(8,128)(2,1)S(1)} %shard_map.76.refs_6_.refs_2_), channel_id=1, source_target_pairs={{0,8},{4,12},{8,0},{12,4},{1,9},{5,13},{9,1},{13,5},{2,10},{6,14},... | collective-permute-start | bytes 786440 | tf_op jit(solution)/shard_map/ppermute | solution.py:406
  37.1 21.7 %collective-permute-start.10 = (bf16[256,1536]{1,0:T(8,128)(2,1)S(1)}, bf16[256,1536]{1,0:T(8,128)(2,1)S(1)}, u32[]{:S(2)}, u32[]{:S(2)}) collective-permute-start(bf16[256,1536]{1,0:T(8,128)(2,1)S(1)} %get-tuple-element.43.refs_6_), channel_id=1, source_target_pairs={{0,1},{1,0},{2,3},{3,2},{4,5},{5,4},{6,7},{7,6},{8,9},{9,8},{10,11... | collective-permute-start | bytes 2359304 | tf_op jit(solution)/shard_map/ppermute | solution.py:383
  45.3 7.7 %collective-permute-start.4 = (bf16[256,1024]{1,0:T(8,128)(2,1)S(1)}, bf16[256,1024]{1,0:T(8,128)(2,1)S(1)}, u32[]{:S(2)}, u32[]{:S(2)}) collective-permute-start(bf16[256,1024]{1,0:T(8,128)(2,1)S(1)} %get-tuple-element.47), channel_id=1, source_target_pairs={{0,1},{1,0},{2,3},{3,2},{4,5},{5,4},{6,7},{7,6},{8,9},{9,8},{10,11... | collective-permute-start | bytes 1572872 | tf_op jit(solution)/shard_map/ppermute | solution.py:383
  46.0 2.7 %collective-permute-start.5 = (bf16[256,1536]{1,0:T(8,128)(2,1)S(1)}, bf16[256,1536]{1,0:T(8,128)(2,1)S(1)}, u32[]{:S(2)}, u32[]{:S(2)}) collective-permute-start(bf16[256,1536]{1,0:T(8,128)(2,1)S(1)} %get-tuple-element.48.refs_3_), channel_id=1, source_target_pairs={{0,1},{1,0},{2,3},{3,2},{4,5},{5,4},{6,7},{7,6},{8,9},{9,8},{10,11... | collective-permute-start | bytes 2359304 | tf_op jit(solution)/shard_map/ppermute | solution.py:383
  47.4 20.9 %collective-permute-start.9 = (bf16[768,256]{1,0:T(8,128)(2,1)S(1)}, bf16[768,256]{1,0:T(8,128)(2,1)S(1)}, u32[]{:S(2)}, u32[]{:S(2)}) collective-permute-start(bf16[768,256]{1,0:T(8,128)(2,1)S(1)} %get-tuple-element.50.refs_1_.refs_2_), channel_id=1, source_target_pairs={{0,8},{4,12},{8,0},{12,4},{1,9},{5,13},{9,1},{13,5},{2,10},{6,14},... | collective-permute-start | bytes 1179656 | tf_op jit(solution)/shard_map/ppermute | solution.py:406
  56.3 11.9 %collective-permute-start.8 = (bf16[256,512]{1,0:T(8,128)(2,1)S(1)}, bf16[256,512]{1,0:T(8,128)(2,1)S(1)}, u32[]{:S(2)}, u32[]{:S(2)}) collective-permute-start(bf16[256,512]{1,0:T(8,128)(2,1)S(1)} %get-tuple-element.53), channel_id=1, source_target_pairs={{0,2},{1,3},{2,0},{3,1},{4,6},{5,7},{6,4},{7,5},{8,10},{9,11},{10,... | collective-permute-start | bytes 786440 | tf_op jit(solution)/shard_map/ppermute | solution.py:391
  58.7 12.1 %collective-permute-start.3 = (bf16[256,1024]{1,0:T(8,128)(2,1)S(1)}, bf16[256,1024]{1,0:T(8,128)(2,1)S(1)}, u32[]{:S(2)}, u32[]{:S(2)}) collective-permute-start(bf16[256,1024]{1,0:T(8,128)(2,1)S(1)} %get-tuple-element.45), channel_id=1, source_target_pairs={{0,1},{1,0},{2,3},{3,2},{4,5},{5,4},{6,7},{7,6},{8,9},{9,8},{10,11... | collective-permute-start | bytes 1572872 | tf_op jit(solution)/shard_map/ppermute | solution.py:383
  63.1 13.4 %collective-permute-start.12 = (bf16[256,768]{1,0:T(8,128)(2,1)S(1)}, bf16[256,768]{1,0:T(8,128)(2,1)S(1)}, u32[]{:S(2)}, u32[]{:S(2)}) collective-permute-start(bf16[256,768]{1,0:T(8,128)(2,1)S(1)} %get-tuple-element.60), channel_id=1, source_target_pairs={{0,2},{1,3},{2,0},{3,1},{4,6},{5,7},{6,4},{7,5},{8,10},{9,11},{10,... | collective-permute-start | bytes 1179656 | tf_op jit(solution)/shard_map/ppermute | solution.py:391
  63.5 20.0 %collective-permute-start.14 = (bf16[256,768]{1,0:T(8,128)(2,1)S(1)}, bf16[256,768]{1,0:T(8,128)(2,1)S(1)}, u32[]{:S(2)}, u32[]{:S(2)}) collective-permute-start(bf16[256,768]{1,0:T(8,128)(2,1)S(1)} %get-tuple-element.62), channel_id=1, source_target_pairs={{0,2},{1,3},{2,0},{3,1},{4,6},{5,7},{6,4},{7,5},{8,10},{9,11},{10,... | collective-permute-start | bytes 1179656 | tf_op jit(solution)/shard_map/ppermute | solution.py:391
  69.6 14.0 %collective-permute-start.15 = (bf16[512,256]{1,0:T(8,128)(2,1)S(1)}, bf16[512,256]{1,0:T(8,128)(2,1)S(1)}, u32[]{:S(2)}, u32[]{:S(2)}) collective-permute-start(bf16[512,256]{1,0:T(8,128)(2,1)S(1)} %get-tuple-element.56.refs_1_), channel_id=1, source_target_pairs={{0,12},{4,0},{8,4},{12,8},{1,13},{5,1},{9,5},{13,9},{2,14},{6,2},{... | collective-permute-start | bytes 786440 | tf_op jit(solution)/shard_map/ppermute | solution.py:406
  74.1 14.6 %collective-permute-start.11 = (bf16[256,512]{1,0:T(8,128)(2,1)S(1)}, bf16[256,512]{1,0:T(8,128)(2,1)S(1)}, u32[]{:S(2)}, u32[]{:S(2)}) collective-permute-start(bf16[256,512]{1,0:T(8,128)(2,1)S(1)} %get-tuple-element.58), channel_id=1, source_target_pairs={{0,2},{1,3},{2,0},{3,1},{4,6},{5,7},{6,4},{7,5},{8,10},{9,11},{10,... | collective-permute-start | bytes 786440 | tf_op jit(solution)/shard_map/ppermute | solution.py:391
  77.6 11.1 %collective-permute-start.13 = (bf16[768,256]{1,0:T(8,128)(2,1)S(1)}, bf16[768,256]{1,0:T(8,128)(2,1)S(1)}, u32[]{:S(2)}, u32[]{:S(2)}) collective-permute-start(bf16[768,256]{1,0:T(8,128)(2,1)S(1)} %get-tuple-element.61.refs_4_), channel_id=1, source_target_pairs={{0,12},{4,0},{8,4},{12,8},{1,13},{5,1},{9,5},{13,9},{2,14},{6,2},{... | collective-permute-start | bytes 1179656 | tf_op jit(solution)/shard_map/ppermute | solution.py:406
  85.2 13.9 %collective-permute-start.17 = (bf16[768,256]{1,0:T(8,128)(2,1)S(1)}, bf16[768,256]{1,0:T(8,128)(2,1)S(1)}, u32[]{:S(2)}, u32[]{:S(2)}) collective-permute-start(bf16[768,256]{1,0:T(8,128)(2,1)S(1)} %get-tuple-element.65.refs_4_), channel_id=1, source_target_pairs={{0,4},{4,8},{8,12},{12,0},{1,5},{5,9},{9,13},{13,1},{2,6},{6,10},{... | collective-permute-start | bytes 1179656 | tf_op jit(solution)/shard_map/ppermute | solution.py:406
  90.1 12.8 %collective-permute-start.16 = (bf16[512,256]{1,0:T(8,128)(2,1)S(1)}, bf16[512,256]{1,0:T(8,128)(2,1)S(1)}, u32[]{:S(2)}, u32[]{:S(2)}) collective-permute-start(bf16[512,256]{1,0:T(8,128)(2,1)S(1)} %get-tuple-element.67.refs_1_), channel_id=1, source_target_pairs={{0,4},{4,8},{8,12},{12,0},{1,5},{5,9},{9,13},{13,1},{2,6},{6,10},{... | collective-permute-start | bytes 786440 | tf_op jit(solution)/shard_map/ppermute | solution.py:406
